TPU v7x, 256 devices: a whole 4x4x8 slice. The times are simulated.
256 devices in a mesh: gx: 32 (over y, x, core), gy: 8 (over z).
Axes of the slice: x: 4, y: 4, z: 8, core: 2. Of those that a mesh axis runs over, the one named last changes fastest.
Arguments:
- grid_field: float32 [2, 64, 1024, 2048], P(None, None, 'gx', 'gy'), may hold values from -6 to 6
- coefficient: float32 [1024, 2048], P('gx', 'gy'), may hold values from 0.5 to 2
- spectral_weight: float32 [128, 128, 64, 128], P('gx', 'gy'), may hold values from -0.5 to 0.5
- local_weight: float32 [64, 64], replicated, may hold values from -0.75 to 0.75
Outputs:
- layer_out: float32 [2, 64, 1024, 2048], P(None, None, 'gx', 'gy')
All inputs are finite; a program needn't handle non-finite values.
Results may differ from a plain program's by a relative error of at most 0.00005.
Values sent between devices are 32-bit elements; how exact they have to be, the bound alone decides.
A program may use at most 128 MiB of HBM per device.

v0:
```python
import math

import jax
import jax.numpy as jnp
from jax import lax
from jax.sharding import PartitionSpec as P

MX = 128


highest = lax.Precision.HIGHEST


def padded_2(block, sides, width):
    for axis, dim in sides:
        count = lax.axis_size(axis)
        forward = [(i, i + 1) for i in range(count - 1)]
        backward = [(target, source) for source, target in forward]
        low = lax.ppermute(
            lax.slice_in_dim(block, block.shape[dim] - width, None, axis=dim), axis, forward
        )
        high = lax.ppermute(lax.slice_in_dim(block, 0, width, axis=dim), axis, backward)
        block = jnp.concatenate([low, block, high], axis=dim)
    return block


def phases(position, frequency, period):
    product = position[:, None] * frequency[None, :] % period
    return product.astype(jnp.float32) * (2.0 * math.pi / period)


def signed_modes(index_range, count, period):
    return jnp.where(index_range < count // 2, index_range, index_range - count + period)


def synthesize(x_position, frequency, total_rows, piece):
    x_angle = phases(x_position, frequency, total_rows)
    x_cosine = jnp.cos(x_angle)
    x_sine = jnp.sin(x_angle)
    real_part = jnp.einsum("xk,kmbo->xmbo", x_cosine, piece[:, 0], precision=highest) - jnp.einsum(
        "xk,kmbo->xmbo", x_sine, piece[:, 1], precision=highest
    )
    imag_part = jnp.einsum("xk,kmbo->xmbo", x_sine, piece[:, 0], precision=highest) + jnp.einsum(
        "xk,kmbo->xmbo", x_cosine, piece[:, 1], precision=highest
    )
    return jnp.stack([real_part, imag_part], axis=1)


def shards(grid_field, coefficient, spectral_weight, local_weight):
    rows_here = grid_field.shape[2]
    cols_here = grid_field.shape[3]
    total_rows = rows_here * lax.axis_size("gx")
    total_cols = cols_here * lax.axis_size("gy")
    modes_x_here = spectral_weight.shape[0]
    modes_y_here = spectral_weight.shape[1]
    channels = local_weight.shape[0]
    y_position = lax.axis_index("gy") * cols_here + jnp.arange(cols_here, dtype=jnp.int32)
    x_position = lax.axis_index("gx") * rows_here + jnp.arange(rows_here, dtype=jnp.int32)
    y_angle = phases(
        y_position, jnp.arange(lax.axis_size("gy") * modes_y_here, dtype=jnp.int32), total_cols
    )
    real_part = jnp.einsum("bcxy,yk->kbcx", grid_field, jnp.cos(y_angle), precision=highest)
    imag_part = -jnp.einsum("bcxy,yk->kbcx", grid_field, jnp.sin(y_angle), precision=highest)
    y_modes = lax.psum_scatter(
        jnp.stack([real_part, imag_part], axis=1), "gy", scatter_dimension=0, tiled=True
    )
    y_real = y_modes[:, 0]
    y_imag = y_modes[:, 1]
    frequency = signed_modes(
        jnp.arange(lax.axis_size("gx") * modes_x_here, dtype=jnp.int32), MX, total_rows
    )
    x_angle = phases(x_position, frequency, total_rows)
    x_cosine = jnp.cos(x_angle)
    x_sine = jnp.sin(x_angle)
    real_part = jnp.einsum("xk,mbcx->kmbc", x_cosine, y_real, precision=highest) + jnp.einsum(
        "xk,mbcx->kmbc", x_sine, y_imag, precision=highest
    )
    imag_part = jnp.einsum("xk,mbcx->kmbc", x_cosine, y_imag, precision=highest) - jnp.einsum(
        "xk,mbcx->kmbc", x_sine, y_real, precision=highest
    )
    z_modes = lax.psum_scatter(
        jnp.stack([real_part, imag_part], axis=1), "gx", scatter_dimension=0, tiled=True
    )
    z_real = z_modes[:, 0]
    z_imag = z_modes[:, 1]
    w_real = spectral_weight[..., :channels]
    w_imag = spectral_weight[..., channels:]
    m_real = jnp.einsum("kmbi,kmio->kmbo", z_real, w_real, precision=highest) - jnp.einsum(
        "kmbi,kmio->kmbo", z_imag, w_imag, precision=highest
    )
    m_imag = jnp.einsum("kmbi,kmio->kmbo", z_real, w_imag, precision=highest) + jnp.einsum(
        "kmbi,kmio->kmbo", z_imag, w_real, precision=highest
    )
    mixed = jnp.stack([m_real, m_imag], axis=1)
    piece = lax.all_gather(mixed, "gx", axis=0, tiled=True)
    frequency = signed_modes(jnp.arange(piece.shape[0], dtype=jnp.int32), MX, total_rows)
    g_modes = synthesize(x_position, frequency, total_rows, piece)
    scale_total = float(total_rows * total_cols)
    piece = lax.all_gather(g_modes, "gy", axis=2, tiled=True)
    frequency = jnp.arange(piece.shape[2], dtype=jnp.int32)
    y_angle = phases(y_position, frequency, total_cols)
    y_weights = jnp.where(frequency == 0, 1.0, 2.0).astype(jnp.float32) / scale_total
    cosine_weighted = jnp.cos(y_angle) * y_weights[None, :]
    sine_weighted = jnp.sin(y_angle) * y_weights[None, :]
    spectral = jnp.einsum(
        "xmbo,ym->boxy", piece[:, 0], cosine_weighted, precision=highest
    ) - jnp.einsum("xmbo,ym->boxy", piece[:, 1], sine_weighted, precision=highest)
    padded = padded_2(grid_field, (("gx", 2), ("gy", 3)), 1)
    beside_all = (
        padded[:, :, 2:, 1:-1]
        + padded[:, :, :-2, 1:-1]
        + padded[:, :, 1:-1, 2:]
        + padded[:, :, 1:-1, :-2]
    )
    stencil = coefficient * (grid_field - 0.25 * beside_all)
    pointwise = jnp.einsum("oi,bixy->boxy", local_weight, grid_field, precision=highest)
    return jax.nn.gelu(spectral + pointwise + stencil)


def solution(mesh):
    placed = (P(None, None, "gx", "gy"), P("gx", "gy"), P("gx", "gy", None, None), P())
    return jax.shard_map(
        shards, mesh=mesh, in_specs=placed, out_specs=P(None, None, "gx", "gy"), check_vma=False
    )
```

profile of v0, /device:TPU:1, one launch (start us, length us, event | category | flops | bytes accessed | tf_op | source)
XLA Modules:
  0.0 472.1 jit_solution(10843069374846154380)
XLA Ops:
  6.5 0.0 copy-start
  6.5 9.0 %fusion.26 = f32[128,1,2,64,32]{0,3,4,2,1:T(8,128)S(1)} fusion(f32[2,64,32,256]{3,2,1,0:T(8,128)} %param.4, s32[256]{0:T(256)S(1)} %iota_add_fusion), kind=kOutput, calls=%fused_computation.39 | convolution fusion | flops 1611071488 | bytes 6292480 | tf_op jit(solution)/shard_map/bcxy,yk->kbcx/dot_general | solution.py:62
  15.5 0.0 copy-done.1
  15.5 5.8 %negate_bitcast_fusion = f32[128,1,2,64,32]{0,3,4,2,1:T(8,128)S(1)} fusion(f32[2,64,32,256]{3,2,1,0:T(8,128)S(1)} %copy-done.1, s32[256]{0:T(256)S(1)} %iota_add_fusion), kind=kOutput, calls=%fused_computation.30 | convolution fusion | flops 1611595776 | bytes 6292480 | tf_op jit(solution)/shard_map/bcxy,yk->kbcx/dot_general | solution.py:63
  21.3 2.3 pad_maximum_fusion.4
  23.7 9.2 %copy.32 = f32[128,2,2,64,32]{3,4,2,1,0:T(8,128)} copy(f32[128,2,2,64,32]{0,3,4,2,1:T(8,128)} %pad_maximum_fusion.4) | data formatting | bytes 8388608 | tf_op jit(solution)/shard_map/stack | solution.py:65
  32.9 0.0 reduce-scatter.3.cloned.1.call-update
  32.9 0.3 reduce-scatter.5.cloned.1.call-start
  33.2 98.6 %reduce-scatter.3.cloned.1.call-done = f32[16,2,2,64,32]{3,4,2,1,0:T(8,128)} async-done(((f32[128,2,2,64,32]{3,4,2,1,0:T(8,128)}), f32[16,2,2,64,32]{3,4,2,1,0:T(8,128)}) %reduce-scatter.3.cloned.1.call-update) | async-done | bytes 524304 | tf_op jit(solution)/shard_map/reduce_scatter | solution.py:64
  131.8 3.0 fusion.48
  134.8 2.9 fusion.47
  137.7 2.9 fusion.31
  140.6 1.9 fusion.32
  142.5 1.5 pad_maximum_fusion.5
  144.0 5.7 %copy.35 = f32[128,2,16,2,64]{4,2,3,1,0:T(8,128)} copy(f32[128,2,16,2,64]{0,4,3,2,1:T(8,128)} %pad_maximum_fusion.5) | data formatting | bytes 4194304 | tf_op jit(solution)/shard_map/stack | solution.py:82
  149.7 0.0 reduce-scatter.5.cloned.1.call-update
  149.7 0.4 all-gather.3.cloned.1.call-start
  150.2 86.2 %reduce-scatter.5.cloned.1.call-done = f32[4,2,16,2,64]{4,2,3,1,0:T(8,128)} async-done(((f32[128,2,16,2,64]{4,2,3,1,0:T(8,128)}), f32[4,2,16,2,64]{4,2,3,1,0:T(8,128)}) %reduce-scatter.5.cloned.1.call-update) | async-done | bytes 65552 | tf_op jit(solution)/shard_map/reduce_scatter | solution.py:81
  236.3 0.9 fusion.144
  237.2 2.1 fusion.20
  239.4 2.1 fusion.18
  241.5 1.9 fusion.38
  243.3 1.9 fusion.44
  245.2 0.7 pad_maximum_fusion.7
  245.9 0.0 all-gather.3.cloned.1.call-update
  246.0 0.0 all-gather.5.cloned.1.call-start
  246.0 52.7 %all-gather.3.cloned.1.call-done = f32[128,2,16,2,64]{4,3,2,0,1:T(2,128)} async-done(((f32[4,2,16,2,64]{4,3,2,0,1:T(2,128)}), f32[128,2,16,2,64]{4,3,2,0,1:T(2,128)}) %all-gather.3.cloned.1.call-update) | async-done | bytes 2097168 | tf_op jit(solution)/shard_map/all_gather | solution.py:95
  298.7 5.4 %slice_bitcast_fusion.2 = (f32[128,16,2,64]{3,2,1,0:T(2,128)S(1)}, f32[128,16,2,64]{3,2,1,0:T(2,128)}) fusion(f32[128,2,16,2,64]{4,3,2,0,1:T(2,128)} %all-gather.3.cloned.1.call-done), kind=kLoop, calls=%fused_computation.27 | loop fusion | bytes 4194304 | tf_op jit(solution)/shard_map/squeeze | solution.py:41
  304.1 2.9 copy.38
  307.0 3.6 fusion.73
  310.7 3.6 fusion.79
  314.3 1.0 copy.39
  315.3 3.9 fusion.34
  319.2 3.8 fusion.33
  323.1 1.1 pad_maximum_fusion.6
  324.2 0.0 all-gather.5.cloned.1.call-update
  324.2 0.0 copy-start.2
  324.2 4.8 %copy.61 = f32[2,64,32,256]{3,1,0,2:T(8,128)S(1)} copy(f32[2,64,32,256]{3,2,1,0:T(8,128)} %param.4) | data formatting | bytes 8388608 | tf_op args[0]
  329.0 0.0 copy-start.4
  329.0 2.9 collective-permute-start.1
  332.0 1.9 collective-permute-start
  333.9 0.0 collective-permute-done.1
  333.9 2.7 constant_dynamic-update-slice_fusion.1
  336.7 2.0 collective-permute-done
  338.7 2.7 fusion.142
  341.4 0.1 copy-done.6
  341.5 2.4 copy.51
  343.9 0.7 copy.53
  344.7 3.2 collective-permute-start.3
  347.8 1.5 collective-permute-start.2
  349.3 4.3 collective-permute-done.2
  353.6 2.1 copy.52
  355.8 0.0 collective-permute-done.3
  355.8 2.1 copy.54
  357.9 59.6 %all-gather.5.cloned.1.call-done = f32[32,2,128,2,64]{4,0,3,2,1:T(8,128)} async-done(((f32[32,2,16,2,64]{4,0,3,2,1:T(8,128)}), f32[32,2,128,2,64]{4,0,3,2,1:T(8,128)}) %all-gather.5.cloned.1.call-update) | async-done | bytes 4194320 | tf_op jit(solution)/shard_map/all_gather | solution.py:99
  417.5 8.6 %slice_bitcast_fusion = (f32[32,128,2,64]{3,0,2,1:T(8,128)}, f32[32,128,2,64]{3,0,2,1:T(8,128)}) fusion(f32[32,2,128,2,64]{4,0,3,2,1:T(8,128)} %all-gather.5.cloned.1.call-done), kind=kLoop, calls=%fused_computation.19 | loop fusion | bytes 8388608 | tf_op jit(solution)/shard_map/squeeze | solution.py:107
  426.1 4.8 %copy.43 = f32[32,128,2,64]{1,3,2,0:T(8,128)} copy(f32[32,128,2,64]{3,0,2,1:T(8,128)} %get-tuple-element.5) | data formatting | bytes 4194304 | tf_op jit(solution)/shard_map/squeeze | solution.py:107
  430.9 3.8 copy.42
  434.7 7.5 %fusion.54 = f32[256,4096]{0,1} fusion(f32[128,4096]{0,1:T(8,128)} %bitcast.101, f32[128]{0:T(128)S(1)} %fusion.93, s32[256]{0:T(256)S(1)} %iota_add_fusion), kind=kOutput, calls=%fused_computation.66 | convolution fusion | flops 1611104256 | bytes 6292992
  442.2 6.1 %fusion.56 = f32[256,4096]{0,1} fusion(f32[128,4096]{0,1:T(8,128)S(1)} %bitcast.100, f32[128]{0:T(128)S(1)} %fusion.93, s32[256]{0:T(256)S(1)} %iota_add_fusion), kind=kOutput, calls=%fused_computation.68 | convolution fusion | flops 1611104256 | bytes 6292992
  448.3 0.0 copy-done
  448.4 0.0 copy-done.8
  448.4 12.3 %fusion.6 = f32[2,64,32,256]{3,1,0,2:T(8,128)S(1)} fusion(f32[2,64,32,256]{3,1,0,2:T(8,128)S(1)} %copy-done.5, f32[2,64,34,256]{3,1,0,2:T(8,128)} %copy-done.6, f32[2,64,34,1]{3,1,0,2:T(8,128)} %copy.54, f32[2,64,34,1]{3,1,0,2:T(8,128)} %copy.52, f32[2,64,1,256]{3,1,0,2:T(8,128)S(1)} %collective-permute-done.1, ...), kind=kOutput, calls=%fused_computation.7 | convolution fusion | flops 827326464 | bytes 21579776 | tf_op jit(solution)/shard_map/oi,bixy->boxy/dot_general | solution.py:116
  460.6 4.4 copy.56
  (19 shorter events, 0.1 us)
Async XLA Ops:
  6.5 441.8 %copy-start = (f32[64,64]{1,0:T(8,128)S(1)}, f32[64,64]{1,0:T(8,128)}, u32[]{:S(2)}) copy-start(f32[64,64]{1,0:T(8,128)} %param.7) | copy-start | bytes 49156
  6.5 125.3 %reduce-scatter.3.cloned.1.call-start = ((), (), s32[]{:S(2)}) async-start(), calls=%async_computation.2 | async-start | bytes 9437184 | tf_op jit(solution)/shard_map/reduce_scatter | solution.py:64
  6.5 9.0 %copy-start.1 = (f32[2,64,32,256]{3,2,1,0:T(8,128)S(1)}, f32[2,64,32,256]{3,2,1,0:T(8,128)}, u32[]{:S(2)}) copy-start(f32[2,64,32,256]{3,2,1,0:T(8,128)} %param.4) | copy-start | bytes 12582916
  32.9 203.4 %reduce-scatter.5.cloned.1.call-start = ((), (), s32[]{:S(2)}) async-start(), calls=%async_computation.3 | async-start | bytes 4325376 | tf_op jit(solution)/shard_map/reduce_scatter | solution.py:81
  131.8 8.8 %copy-start.7 = (f32[16,2,2,64,32]{3,4,2,1,0:T(8,128)S(1)}, f32[16,2,2,64,32]{3,4,2,1,0:T(8,128)}, u32[]{:S(2)}) copy-start(f32[16,2,2,64,32]{3,4,2,1,0:T(8,128)} %reduce-scatter.3.cloned.1.call-done) | copy-start | bytes 1572868
  144.0 93.2 %copy-start.3 = (f32[4,16,64,128]{3,2,1,0:T(8,128)S(1)}, f32[4,16,64,128]{3,2,1,0:T(8,128)}, u32[]{:S(2)}) copy-start(f32[4,16,64,128]{3,2,1,0:T(8,128)} %param.6) | copy-start | bytes 6291460
  149.7 149.0 %all-gather.3.cloned.1.call-start = ((), (), s32[]{:S(2)}) async-start(), calls=%async_computation.4 | async-start | bytes 4325376 | tf_op jit(solution)/shard_map/all_gather | solution.py:95
  246.0 171.5 %all-gather.5.cloned.1.call-start = ((), (), s32[]{:S(2)}) async-start(), calls=%async_computation.5 | async-start | bytes 9437184 | tf_op jit(solution)/shard_map/all_gather | solution.py:99
  324.2 9.7 %copy-start.2 = (f32[2,64,32,256]{3,2,1,0:T(8,128)S(1)}, f32[2,64,32,256]{3,2,1,0:T(8,128)}, u32[]{:S(2)}) copy-start(f32[2,64,32,256]{3,2,1,0:T(8,128)} %param.4) | copy-start | bytes 12582916
  329.0 7.7 %copy-start.4 = (f32[2,64,32,256]{3,1,0,2:T(8,128)}, f32[2,64,32,256]{3,1,0,2:T(8,128)S(1)}, u32[]{:S(2)}) copy-start(f32[2,64,32,256]{3,1,0,2:T(8,128)S(1)} %copy.61) | copy-start | bytes 12582916
  329.0 4.9 %collective-permute-start.1 = (f32[2,64,1,256]{3,1,0,2:T(8,128)S(1)}, f32[2,64,1,256]{3,1,0,2:T(8,128)S(1)}, u32[]{:S(2)}, u32[]{:S(2)}) collective-permute-start(f32[2,64,1,256]{3,1,0,2:T(8,128)S(1)} %get-tuple-element.12), channel_id=1, source_target_pairs={{0,8},{8,16},{16,24},{24,32},{32,40},{40,48},{48,56},{56,64},{64,7... | collective-permute-start | bytes 393224 | tf_op jit(solution)/shard_map/ppermute | solution.py:19
  332.0 6.7 %collective-permute-start = (f32[2,64,1,256]{3,1,0,2:T(8,128)S(1)}, f32[2,64,1,256]{3,1,0,2:T(8,128)S(1)}, u32[]{:S(2)}, u32[]{:S(2)}) collective-permute-start(f32[2,64,1,256]{3,1,0,2:T(8,128)S(1)} %get-tuple-element.11), channel_id=1, source_target_pairs={{8,0},{16,8},{24,16},{32,24},{40,32},{48,40},{56,48},{64,56},{72,6... | collective-permute-start | bytes 393224 | tf_op jit(solution)/shard_map/ppermute | solution.py:22
  338.7 2.8 copy-start.6
  344.7 11.1 %collective-permute-start.3 = (f32[2,64,34,1]{1,0,3,2:T(2,128)S(1)}, f32[2,64,34,1]{1,0,3,2:T(2,128)S(1)}, u32[]{:S(2)}, u32[]{:S(2)}) collective-permute-start(f32[2,64,34,1]{1,0,3,2:T(2,128)S(1)} %copy.53), channel_id=1, source_target_pairs={{0,1},{1,2},{2,3},{3,4},{4,5},{5,6},{6,7},{8,9},{9,10},{10,11},{11... | collective-permute-start | bytes 52232 | tf_op jit(solution)/shard_map/ppermute | solution.py:19
  347.8 5.8 %collective-permute-start.2 = (f32[2,64,34,1]{1,0,3,2:T(2,128)S(1)}, f32[2,64,34,1]{1,0,3,2:T(2,128)S(1)}, u32[]{:S(2)}, u32[]{:S(2)}) collective-permute-start(f32[2,64,34,1]{1,0,3,2:T(2,128)S(1)} %copy.51), channel_id=1, source_target_pairs={{1,0},{2,1},{3,2},{4,3},{5,4},{6,5},{7,6},{9,8},{10,9},{11,10},{12... | collective-permute-start | bytes 52232 | tf_op jit(solution)/shard_map/ppermute | solution.py:22
  442.2 6.1 %copy-start.5 = (f32[2,64,32,256]{3,1,0,2:T(8,128)S(1)}, f32[2,64,32,256]{3,1,0,2:T(8,128)}, u32[]{:S(2)}) copy-start(f32[2,64,32,256]{3,1,0,2:T(8,128)} %copy-done.4) | copy-start | bytes 12582916
  442.2 6.1 %copy-start.8 = (f32[32,256]{1,0:T(8,128)S(1)}, f32[32,256]{1,0:T(8,128)}, u32[]{:S(2)}) copy-start(f32[32,256]{1,0:T(8,128)} %param.5) | copy-start | bytes 98308
Sparse Core Ops, SparseCore 0:
  33.0 98.7 reduce-scatter.2
  149.8 86.4 reduce-scatter.4
  246.1 52.5 all-gather.2
  324.3 93.1 all-gather.4
where the time goes:
time: 481 us; the launch traced here: 472 us
  waiting for transfers between devices  303 us (63%)
  matrix products  74.3 us (15%)
  local copies, waits for them, and re-layouts  64.6 us (13%)
  between operations  13.8 us (3%)
  starting transfers between devices  10.3 us (2%)
  other arithmetic  5.69 us (1%)
    reduce_scatter x1, waiting for transfers between devices, shards(): lax.psum_scatter(jnp.stack([real_part, imag_part], axis=1), 'gy', scatter...  98.6 us
    reduce_scatter x1, waiting for transfers between devices, shards(): lax.psum_scatter(jnp.stack([real_part, imag_part], axis=1), 'gx', scatter...  86.2 us
    all_gather x1, waiting for transfers between devices, shards(): piece = lax.all_gather(g_modes, 'gy', axis=2, tiled=True)  59.6 us
    all_gather x1, waiting for transfers between devices, shards(): piece = lax.all_gather(mixed, 'gx', axis=0, tiled=True)  52.7 us
    another operation x2, local copies, waits for them, and re-layouts, shards(): jnp.stack([real_part, imag_part], axis=1)  14.9 us
    unnamed x2, matrix products  13.6 us
    squeeze x2, local copies, waits for them, and re-layouts, shards(): piece[:, 1]  13.4 us
    dot_general x1, matrix products, shards(): jnp.einsum('oi,bixy->boxy', local_weight, grid_field, precision=highest)  12.3 us
  transfers between devices with their start and end apart: 8, of which 6 were waited for; matrix products, arithmetic and copies ran while one was open for 4% of the time, Pallas kernels for 0%

commit v1 on v0

v1 whole, which is shorter than its diff:
```python
import functools
import math

import jax
import jax.numpy as jnp
import ml_dtypes
import numpy as np
from jax import lax
from jax.experimental import pallas as pl
from jax.experimental.pallas import tpu as pltpu
from jax.sharding import PartitionSpec as P

MESH = pl.DeviceIdType.MESH
MX = 128
MY = 128
NX = 1024
NY = 2048
highest = lax.Precision.HIGHEST
f32 = jnp.float32
bf16 = jnp.bfloat16


def halves(table):
    table = np.asarray(table, np.float64)
    high = table.astype(np.float32).astype(ml_dtypes.bfloat16)
    low = (table - high.astype(np.float64)).astype(np.float32).astype(ml_dtypes.bfloat16)
    return np.stack([high, low], axis=-3)


def angles(position, frequency, period):
    return (np.outer(position, frequency) % period) * (2.0 * math.pi / period)


def x_frequency():
    k = np.arange(MX)
    return np.where(k < MX // 2, k, k - MX + NX)


def group_rows(axis, place):
    y, x, c, r = np.meshgrid(np.arange(4), np.arange(4), np.arange(2), np.arange(32), indexing="ij")
    row = ((y * 4 + x) * 2 + c) * 32 + r
    return (row[place] if axis == 0 else row[:, place]).reshape(-1)


def tables():
    fx = x_frequency()
    spread = (np.arange(128) % 32) * 4 + np.arange(128) // 32
    x_fwd, x_inv = [], []
    for axis in (0, 1):
        for place in range(4):
            angle = angles(group_rows(axis, place), fx, NX)
            x_fwd.append(np.concatenate([np.cos(angle).T, np.sin(angle).T], 0))
            x_inv.append(np.concatenate([np.cos(angle)[:, spread], np.sin(angle)[:, spread]], 0))
    y_fwd, y_inv_a, y_inv_b = [], [], []
    weight = np.where(np.arange(MY) == 0, 1.0, 2.0) / float(NX * NY)
    for place in range(8):
        angle = angles(place * 256 + np.arange(256), np.arange(MY), NY).T
        cosine, sine = np.cos(angle), np.sin(angle)
        y_fwd.append(
            np.stack([cosine.reshape(8, 16, 256), -sine.reshape(8, 16, 256)], 1).reshape(256, 256)
        )
        cosine, sine = cosine * weight[:, None], -sine * weight[:, None]
        y_inv_a.append(
            np.stack([cosine.reshape(8, 16, 256), sine.reshape(8, 16, 256)], 1).reshape(256, 256)
        )
        y_inv_b.append(np.concatenate([cosine, sine], 0))
    angle = angles(np.arange(NX), fx, NX)
    x_all_fwd = np.concatenate([np.cos(angle), np.sin(angle)], 1)
    x_all_inv = np.concatenate([np.cos(angle)[:, spread].T, np.sin(angle)[:, spread].T], 1)
    return [
        halves(np.stack(x_fwd)),
        halves(np.stack(x_inv)),
        halves(np.stack(y_fwd)),
        halves(np.stack(y_inv_b)),
        halves(x_all_fwd),
        halves(x_all_inv),
        halves(np.stack(y_inv_a)),
    ]


def split(value):
    high = value.astype(bf16)
    return high, (value - high.astype(f32)).astype(bf16)


def dot(a, b, dims):
    return lax.dot_general(a, b, (dims, ((), ())), preferred_element_type=f32)


NN = ((1,), (0,))
NT = ((1,), (1,))
TN = ((0,), (0,))


def dot3(a, b, dims):
    return dot(a[0], b[0], dims) + (dot(a[0], b[1], dims) + dot(a[1], b[0], dims))


def quarters(blocks):
    rows = blocks[0].shape[0]
    lane = lax.broadcasted_iota(jnp.int32, (rows, 128), 1) // 32
    out = []
    for k in range(4):
        result = blocks[k] if k == 0 else None
        for v in range(4):
            shift = (32 * (v - k)) % 128
            moved = blocks[v] if shift == 0 else pltpu.roll(blocks[v], shift, 1)
            result = moved if v == 0 else jnp.where(lane == v, moved, result)
        out.append(result)
    return out


class Place:
    def __init__(self):
        self.j = lax.axis_index("gx")
        self.d = lax.axis_index("gy")
        self.y = self.j // 8
        self.x = (self.j // 2) % 4
        self.c = self.j % 2

    def gx(self, r):
        return (
            ((self.y + r // 8) % 4) * 8 + ((self.x + (r // 2) % 4) % 4) * 2 + (self.c + r % 2) % 2
        )

    def gx_back(self, r):
        return (
            ((self.y + 4 - r // 8) % 4) * 8
            + ((self.x + 4 - (r // 2) % 4) % 4) * 2
            + (self.c + r % 2) % 2
        )

    def member(self, axis, r):
        core = (self.c + r % 2) % 2
        if axis == 0:
            place = (self.x + r // 2) % 4
            return place, core, self.y * 8 + place * 2 + core
        place = (self.y + r // 2) % 4
        return place, core, place * 8 + self.x * 2 + core

    def across(self, axis, r):
        if axis == 0:
            place = (self.y + r) % 4
            return place, place * 8 + self.x * 2 + self.c
        place = (self.x + r) % 4
        return place, self.y * 8 + place * 2 + self.c

    def gy(self, r):
        return (self.d + r + 8) % 8


CHAINS = ((1, 0, 4), (-1, 1, 4), (-1, 0, 3), (1, 1, 3))


def spectral_kernel(
    grid,
    weight,
    t_xf,
    t_xi,
    t_yf,
    t_yi,
    t_xaf,
    t_xai,
    gather,
    spec,
    xf,
    xi,
    yf,
    yi,
    xaf,
    xai,
    w,
    g0,
    part,
    ring,
    first,
    z2,
    z2r,
    z3,
    z3r,
    a_send,
    a_recv,
    m_send,
    m_recv,
    n_send,
    n_recv,
    mixed,
    b_send,
    b_recv,
    h3,
    h3r,
    h2r,
    out1,
    load,
    s_p1,
    r_p1,
    s_p2,
    r_p2,
    s_p3,
    r_p3,
    s_ring,
    r_ring,
    s_a,
    r_a,
    s_m,
    r_m,
    s_n,
    r_n,
    s_b,
    r_b,
    s_g,
    r_g,
    s_q3,
    r_q3,
    s_q2,
    r_q2,
    s_q1,
    r_q1,
    own,
):
    at = Place()
    j, d = at.j, at.d

    def remote(src, dst, send, recv, gx, gy):
        return pltpu.make_async_remote_copy(
            src_ref=src, dst_ref=dst, send_sem=send, recv_sem=recv, device_id=(gx, gy), device_id_type=MESH
        )

    loads = [
        pltpu.make_async_copy(grid.at[0], g0, load.at[0]),
        pltpu.make_async_copy(t_yf.at[d], yf, load.at[1]),
        pltpu.make_async_copy(t_xf.at[at.y], xf.at[0], load.at[2]),
        pltpu.make_async_copy(t_xf.at[4 + at.x], xf.at[1], load.at[3]),
        pltpu.make_async_copy(t_xaf, xaf, load.at[4]),
        pltpu.make_async_copy(weight, w, load.at[5]),
        pltpu.make_async_copy(t_xai, xai, load.at[6]),
        pltpu.make_async_copy(t_xi.at[at.y], xi.at[0], load.at[7]),
        pltpu.make_async_copy(t_xi.at[4 + at.x], xi.at[1], load.at[8]),
        pltpu.make_async_copy(t_yi.at[d], yi, load.at[9]),
    ]
    for copy in loads:
        copy.start()

    barrier = pltpu.get_barrier_semaphore()

    def greet(r, carry):
        pl.semaphore_signal(barrier, inc=1, device_id=(at.gx(r), d), device_id_type=MESH)
        return carry

    lax.fori_loop(1, 32, greet, 0)
    for r in range(1, 8):
        pl.semaphore_signal(barrier, inc=1, device_id=(j, at.gy(r)), device_id_type=MESH)
    pl.semaphore_wait(barrier, 31 + 7)

    def grid_piece(axis, chunk, place, core):
        if axis == 0:
            return grid.at[1, 0, pl.ds(2 * chunk, 2), place, core]
        return grid.at[1, 1, place, pl.ds(2 * chunk, 2), core]

    def p1(axis, chunk, r):
        place, core, gx = at.member(axis, r)
        mine = (at.x if axis == 0 else at.y) * 2 + at.c
        return remote(
            grid_piece(axis, chunk, place, core),
            first.at[axis, pl.ds(2 * chunk, 2), mine],
            s_p1.at[axis, chunk, r],
            r_p1.at[axis, chunk, r],
            gx,
            d,
        )

    def p1_own(axis, chunk):
        place = at.x if axis == 0 else at.y
        return pltpu.make_async_copy(
            grid_piece(axis, chunk, place, at.c),
            first.at[axis, pl.ds(2 * chunk, 2), place * 2 + at.c],
            own.at[axis, chunk],
        )

    for chunk in range(2):
        for r in (2, 6, 3, 7, 4, 5, 1):
            for axis in range(2):
                p1(axis, chunk, r).start()
        for axis in range(2):
            p1_own(axis, chunk).start()

    loads[0].wait()
    loads[1].wait()

    def columns(half, carry):
        for k in range(4):
            t = half * 8 + 2 * k
            rows = []
            for tile in range(2):
                own_of = t + tile
                for core in range(2):
                    for low in range(2):
                        rows.append(g0[low, own_of // 4, own_of % 4, core])
            block = split(jnp.concatenate(rows, axis=0))
            result = dot3((yf[0], yf[1]), block, NT)
            for e in range(8):
                part[e, half, :, 256 * k : 256 * k + 256] = result[32 * e : 32 * e + 32]
        return carry

    def hop(chain, s):
        direction, half, hops = CHAINS[chain]
        to = at.gy(direction * (hops - s))
        return remote(
            part.at[to, half],
            ring.at[chain, s],
            s_ring.at[chain, s],
            r_ring.at[chain, s],
            j,
            at.gy(direction),
        )

    def collect(s):
        for chain in range(4):
            direction, half, hops = CHAINS[chain]
            if s < hops:
                hop(chain, s).wait_recv()
                to = at.gy(direction * (hops - 1 - s))
                part[to, half] = part[to, half] + ring[chain, s]
                if s + 1 < hops:
                    hop(chain, s + 1).start()

    columns(0, 0)
    for chain in (0, 2):
        hop(chain, 0).start()
    columns(1, 0)
    for chain in (1, 3):
        hop(chain, 0).start()

    loads[2].wait()
    loads[3].wait()

    def modes_of(axis, channel):
        block = split(first[axis, channel].reshape(256, 256))
        rows = split(dot3((xf[axis, 0], xf[axis, 1]), block, NN))
        both = dot3((yf[0], yf[1]), rows, NT)
        for e in range(8):
            cos_y = both[32 * e : 32 * e + 16]
            sin_y = both[32 * e + 16 : 32 * e + 32]
            z2[axis, channel, e, 0] = cos_y[:, :128] + sin_y[:, 128:]
            z2[axis, channel, e, 1] = sin_y[:, :128] - cos_y[:, 128:]

    def p2(axis, r):
        place, gx = at.across(axis, r)
        return remote(
            z2.at[axis, place], z2r.at[axis, r], s_p2.at[axis, r], r_p2.at[axis, r], gx, d
        )

    def forward_chunk(axis, chunk):
        for r in range(1, 8):
            p1(axis, chunk, r).wait_recv()
        p1_own(axis, chunk).wait()

        def one(k, carry):
            modes_of(axis, 2 * chunk + k)
            return carry

        lax.fori_loop(0, 2, one, 0)

    collect(0)
    for axis in range(2):
        forward_chunk(axis, 0)
    collect(1)
    for axis in range(2):
        forward_chunk(axis, 1)
        for r in (1, 3, 2):
            p2(axis, r).start()
    collect(2)

    for axis in range(2):
        for r in range(1, 4):
            p2(axis, r).wait_recv()
        place = at.y if axis == 0 else at.x
        for e in range(8):
            z3[e, axis] = (z2[axis, place, e] + z2r[axis, 1, e]) + (z2r[axis, 2, e] + z2r[axis, 3, e])

    def p3(r):
        to = at.gy(r)
        return remote(z3.at[to], z3r.at[r], s_p3.at[r], r_p3.at[r], j, to)

    for r in (4, 3, 5, 2, 6, 1, 7):
        p3(r).start()
    collect(3)

    lane = lax.broadcasted_iota(jnp.int32, (16, 128), 1)
    for t in range(16):
        here = pl.ds(128 * (t % 8), 128)
        real = part[d, t // 8, 0:16, here]
        imag = part[d, t // 8, 16:32, here]
        a_send[2 * t] = jnp.where(lane < 64, real, pltpu.roll(imag, 64, 1))
        a_send[2 * t + 1] = jnp.where(lane < 64, pltpu.roll(real, 64, 1), imag)

    def spread_copy(send, recv, s_sem, r_sem, r):
        gx = at.gx(r)
        return remote(send.at[gx], recv.at[j], s_sem.at[r], r_sem.at[r], gx, d)

    def spread_start(*refs):
        def start(r, carry):
            spread_copy(*refs, r).start()
            return carry

        lax.fori_loop(1, 32, start, 0)
        send, recv = refs[:2]
        recv[j] = send[j]

    def spread_wait(*refs):
        def wait(r, carry):
            spread_copy(*refs, r).wait_recv()
            return carry

        lax.fori_loop(1, 32, wait, 0)

    a_refs = (a_send, a_recv, s_a, r_a)
    spread_start(*a_refs)

    for r in range(1, 8):
        p3(r).wait_recv()
    stack = []
    for axis in range(2):
        total = z3[d, axis]
        for r in range(1, 8):
            total = total + z3r[r, axis]
        stack.append(total.reshape(32, 128))

    loads[4].wait()
    spread_wait(*a_refs)
    turned = [quarters([a_recv[4 * u + v] for v in range(4)]) for u in range(8)]
    rows = jnp.concatenate(
        [jnp.concatenate([turned[u][k] for u in range(8)], axis=1) for k in range(4)], axis=0
    )
    both = dot3(split(rows), (xaf[0], xaf[1]), NN)
    for half in range(2):
        real = both[16 * half : 16 * half + 16]
        imag = both[32 + 16 * half : 32 + 16 * half + 16]
        stack.append(real[:, :128] + imag[:, 128:])
        stack.append(imag[:, :128] - real[:, 128:])
    modes = jnp.concatenate(stack, axis=0).T
    for owner in range(32):
        m_send[owner] = modes[4 * owner : 4 * owner + 4]

    m_refs = (m_send, m_recv, s_m, r_m)
    spread_start(*m_refs)
    loads[5].wait()
    spread_wait(*m_refs)

    sign = jnp.where(lax.broadcasted_iota(jnp.int32, (8, 128), 1) < 64, -1.0, 1.0)

    def mix(kx, carry):
        held = m_recv[:, kx, :]
        for sample in range(2):
            rows = []
            for ky in range(16):
                from_real = jnp.zeros((32, 128), f32)
                from_imag = jnp.zeros((32, 128), f32)
                for half in range(2):
                    first_lane = (64 if sample == 0 else 0) + 32 * half + ky
                    block = w[kx, ky, 32 * half : 32 * half + 32, :]
                    from_real += held[:, first_lane : first_lane + 1] * block
                    from_imag += held[:, first_lane + 16 : first_lane + 17] * block
                from_real = (from_real[0:8] + from_real[8:16]) + (from_real[16:24] + from_real[24:32])
                from_imag = (from_imag[0:8] + from_imag[8:16]) + (from_imag[16:24] + from_imag[24:32])
                both = from_real + sign * pltpu.roll(from_imag, 64, 1)
                rows.append(jnp.sum(both, axis=0, keepdims=True))
            mixed[pl.ds(64 * sample + 16 * kx, 16), :] = jnp.concatenate(rows, axis=0)
        return carry

    lax.fori_loop(0, 4, mix, 0)
    turned_modes = mixed[...].T
    for k in range(4):
        n_send[:, k, :] = turned_modes[32 * k : 32 * k + 32]

    n_refs = (n_send, n_recv, s_n, r_n)
    spread_start(*n_refs)
    loads[6].wait()
    spread_wait(*n_refs)

    back = jnp.concatenate([n_recv[:, k, :] for k in range(4)], axis=0).T
    by_sample = []
    for sample in range(2):
        by_sample.append(
            quarters([back[64 * sample + 16 * v : 64 * sample + 16 * v + 16] for v in range(4)])
        )

    for axis in range(2):
        for k in range(2):
            h3[axis, k] = by_sample[1][2 * k + axis]

    def q3(r):
        return remote(h3, h3r.at[d], s_q3.at[r], r_q3.at[r], j, at.gy(r))

    for r in (4, 3, 5, 2, 6, 1, 7):
        q3(r).start()
    h3r[d] = h3[...]

    full = dot3(split(jnp.concatenate(by_sample[0], axis=0)), (xai[0], xai[1]), NN)
    real, imag = full[0:32], full[32:64]
    g_real = real[:, :1024] - imag[:, 1024:]
    g_imag = real[:, 1024:] + imag[:, :1024]
    for u in range(8):
        here = slice(128 * u, 128 * u + 128)
        pieces = quarters(
            [g_real[0:16, here], g_real[16:32, here], g_imag[0:16, here], g_imag[16:32, here]]
        )
        for v in range(4):
            b_send[4 * u + v] = pieces[v]
    b_refs = (b_send, b_recv, s_b, r_b)
    spread_start(*b_refs)

    for r in range(1, 8):
        q3(r).wait_recv()

    def q2(axis, r):
        place, gx = at.across(axis, r)
        mine = at.y if axis == 0 else at.x
        return remote(
            h3r.at[:, axis], h2r.at[axis, mine], s_q2.at[axis, r], r_q2.at[axis, r], gx, d
        )

    for r in (1, 3, 2):
        for axis in range(2):
            q2(axis, r).start()
    h2r[0, at.y] = h3r[:, 0]
    h2r[1, at.x] = h3r[:, 1]

    spread_wait(*b_refs)
    for t in range(16):
        even, odd = b_recv[2 * t], b_recv[2 * t + 1]
        here = pl.ds(128 * (t % 8), 128)
        part[d, t // 8, 0:16, here] = jnp.where(lane < 64, even, pltpu.roll(odd, 64, 1))
        part[d, t // 8, 16:32, here] = jnp.where(lane < 64, pltpu.roll(even, 64, 1), odd)

    def lap(chain, s):
        direction, half, hops = CHAINS[chain]
        block = at.gy(-direction * s)
        src = part.at[block, half] if s == 0 else gather.at[block, half]
        return remote(
            src,
            gather.at[block, half],
            s_g.at[chain, s],
            r_g.at[chain, s],
            j,
            at.gy(direction),
        )

    def pass_on(s):
        for chain in range(4):
            hops = CHAINS[chain][2]
            if s < hops:
                lap(chain, s).wait_recv()
                if s + 1 < hops:
                    lap(chain, s + 1).start()

    for chain in range(4):
        lap(chain, 0).start()
    keep = pltpu.make_async_copy(part.at[d], gather.at[d], own.at[0, 0])
    keep.start()

    for k in range(7, 10):
        loads[k].wait()

    def rows_of(axis, channel):
        real = jnp.concatenate([h2r[axis, channel, e, 0] for e in range(8)], axis=0)
        imag = jnp.concatenate([h2r[axis, channel, e, 1] for e in range(8)], axis=0)
        both = dot3((xi[axis, 0], xi[axis, 1]), split(jnp.concatenate([real, imag], axis=0)), NT)
        g_real = both[:256, :128] - both[256:, 128:]
        g_imag = both[256:, :128] + both[:256, 128:]
        wide = split(jnp.concatenate([g_real, g_imag], axis=1))
        out1[axis, channel] = dot3(wide, (yi[0], yi[1]), NN).reshape(8, 32, 256)

    def spec_piece(axis, chunk):
        if axis == 0:
            return spec.at[0, pl.ds(2 * chunk, 2), at.x, at.c]
        return spec.at[1, at.y, pl.ds(2 * chunk, 2), at.c]

    def q1(axis, chunk, r):
        place, core, gx = at.member(axis, r)
        return remote(
            out1.at[axis, pl.ds(2 * chunk, 2), place * 2 + core],
            spec_piece(axis, chunk),
            s_q1.at[axis, chunk, r],
            r_q1.at[axis, chunk, r],
            gx,
            d,
        )

    def q1_own(axis, chunk):
        place = at.x if axis == 0 else at.y
        return pltpu.make_async_copy(
            out1.at[axis, pl.ds(2 * chunk, 2), place * 2 + at.c],
            spec_piece(axis, chunk),
            own.at[axis, 2 + chunk],
        )

    def inverse_chunk(axis, chunk):
        def one(k, carry):
            rows_of(axis, 2 * chunk + k)
            return carry

        lax.fori_loop(0, 2, one, 0)
        for r in (2, 6, 3, 7, 4, 5, 1):
            q1(axis, chunk, r).start()
        q1_own(axis, chunk).start()

    for axis in range(2):
        for r in range(1, 4):
            q2(axis, r).wait_recv()
    for axis in range(2):
        inverse_chunk(axis, 0)
    pass_on(0)
    for axis in range(2):
        inverse_chunk(axis, 1)
    pass_on(1)
    pass_on(2)
    pass_on(3)
    for chunk in range(2):
        for axis in range(2):
            for r in range(1, 8):
                q1(axis, chunk, r).wait_recv()
            q1_own(axis, chunk).wait()
    keep.wait()

    for chunk in range(2):
        for axis in range(2):
            for r in range(1, 8):
                p1(axis, chunk, r).wait_send()
                q1(axis, chunk, r).wait_send()
    for axis in range(2):
        for r in range(1, 4):
            p2(axis, r).wait_send()
            q2(axis, r).wait_send()
    for r in range(1, 8):
        p3(r).wait_send()
        q3(r).wait_send()
    for chain in range(4):
        for s in range(CHAINS[chain][2]):
            hop(chain, s).wait_send()
            lap(chain, s).wait_send()

    def sent(r, carry):
        for refs in (a_refs, m_refs, n_refs, b_refs):
            spread_copy(*refs, r).wait_send()
        return carry

    lax.fori_loop(1, 32, sent, 0)


def spectral_call(grid_field, spectral_weight, consts):
    dma = pltpu.SemaphoreType.DMA
    vmem = pltpu.VMEM
    scratch = [
        vmem((2, 2, 256, 256), bf16),
        vmem((2, 2, 512, 128), bf16),
        vmem((2, 256, 256), bf16),
        vmem((2, 256, 256), bf16),
        vmem((2, 1024, 256), bf16),
        vmem((2, 128, 2048), bf16),
        vmem((4, 16, 64, 128), f32),
        vmem((2, 4, 4, 2, 32, 256), f32),
        vmem((8, 2, 32, 1024), f32),
        vmem((4, 4, 32, 1024), f32),
        vmem((2, 4, 8, 32, 256), f32),
        vmem((2, 4, 8, 2, 16, 128), f32),
        vmem((2, 4, 8, 2, 16, 128), f32),
        vmem((8, 2, 2, 16, 128), f32),
        vmem((8, 2, 2, 16, 128), f32),
        vmem((32, 16, 128), f32),
        vmem((32, 16, 128), f32),
        vmem((32, 4, 128), f32),
        vmem((32, 4, 128), f32),
        vmem((32, 4, 128), f32),
        vmem((32, 4, 128), f32),
        vmem((128, 128), f32),
        vmem((32, 16, 128), f32),
        vmem((32, 16, 128), f32),
        vmem((2, 2, 16, 128), f32),
        vmem((8, 2, 2, 16, 128), f32),
        vmem((2, 4, 8, 2, 16, 128), f32),
        vmem((2, 4, 8, 32, 256), f32),
        dma((10,)),
        dma((2, 2, 8)),
        dma((2, 2, 8)),
        dma((2, 4)),
        dma((2, 4)),
        dma((8,)),
        dma((8,)),
        dma((4, 4)),
        dma((4, 4)),
        *[dma((32,)) for _ in range(8)],
        dma((4, 4)),
        dma((4, 4)),
        dma((8,)),
        dma((8,)),
        dma((2, 4)),
        dma((2, 4)),
        dma((2, 2, 8)),
        dma((2, 2, 8)),
        dma((2, 4)),
    ]
    hbm = pl.BlockSpec(memory_space=pl.ANY)
    return pl.pallas_call(
        spectral_kernel,
        out_shape=(
            jax.ShapeDtypeStruct((8, 2, 32, 1024), f32),
            jax.ShapeDtypeStruct((2, 4, 4, 2, 32, 256), f32),
        ),
        in_specs=[hbm] * 8,
        out_specs=(hbm, hbm),
        scratch_shapes=scratch,
        compiler_params=pltpu.CompilerParams(
            collective_id=0, has_side_effects=True, vmem_limit_bytes=48 << 20
        ),
        name="spectral",
    )(grid_field, spectral_weight, *consts)


def padded_2(block, sides, width):
    for axis, dim in sides:
        count = lax.axis_size(axis)
        forward = [(i, i + 1) for i in range(count - 1)]
        backward = [(target, source) for source, target in forward]
        low = lax.ppermute(
            lax.slice_in_dim(block, block.shape[dim] - width, None, axis=dim), axis, forward
        )
        high = lax.ppermute(lax.slice_in_dim(block, 0, width, axis=dim), axis, backward)
        block = jnp.concatenate([low, block, high], axis=dim)
    return block


def shards(consts, grid_field, coefficient, spectral_weight, local_weight):
    consts = [jnp.asarray(c) for c in consts]
    view = grid_field.reshape(2, 2, 4, 4, 2, 32, 256)
    gather, spec = spectral_call(view, spectral_weight, consts[:6])
    y_inv = consts[6][lax.axis_index("gy")].astype(f32)
    y_inv = y_inv[0] + y_inv[1]
    low = jnp.einsum("dhkl,dky->hly", gather, y_inv.reshape(8, 32, 256), precision=highest)
    low = low.reshape(2, 8, 2, 2, 32, 256)
    low = jnp.transpose(low, (3, 0, 1, 2, 4, 5)).reshape(64, 32, 256)
    spectral = jnp.stack([low, spec.reshape(64, 32, 256)])
    padded = padded_2(grid_field, (("gx", 2), ("gy", 3)), 1)
    beside_all = (
        padded[:, :, 2:, 1:-1]
        + padded[:, :, :-2, 1:-1]
        + padded[:, :, 1:-1, 2:]
        + padded[:, :, 1:-1, :-2]
    )
    stencil = coefficient * (grid_field - 0.25 * beside_all)
    pointwise = jnp.einsum("oi,bixy->boxy", local_weight, grid_field, precision=highest)
    return jax.nn.gelu(spectral + pointwise + stencil)


def solution(mesh):
    consts = tables()
    placed = (P(None, None, "gx", "gy"), P("gx", "gy"), P("gx", "gy", None, None), P())
    return jax.shard_map(
        functools.partial(shards, consts),
        mesh=mesh,
        in_specs=placed,
        out_specs=P(None, None, "gx", "gy"),
        check_vma=False,
    )
```

time: 481 us -> 214 us (0.44); the launches traced: 472 us -> 210 us
  waiting for transfers between devices: 303 us -> 0.01 us
  Pallas kernels: 0 us -> 123 us
  matrix products: 74.3 us -> 34.9 us
  local copies, waits for them, and re-layouts: 64.6 us -> 40.5 us
  between operations: 13.8 us -> 0.43 us
    reduce_scatter x2 -> x0, waiting for transfers between devices: 185 us -> none  [the longest x1 98.6 us: shards(): lax.psum_scatter(jnp.stack([real_part, imag_part], axis=1), 'gy', scatter...]
    pallas_call x0 -> x1, Pallas kernels: none -> 123 us  [spectral_call(): pl.pallas_call(spectral_kernel, out_shape=(jax.ShapeDtypeStruct((8, 2, 32...]
    all_gather x2 -> x0, waiting for transfers between devices: 112 us -> none  [the longest x1 59.6 us: shards(): piece = lax.all_gather(g_modes, 'gy', axis=2, tiled=True)]
    dot_general x14 -> x1, matrix products: 48.4 us -> 20.2 us  [shards(): jnp.einsum('dhkl,dky->hly', gather, y_inv.reshape(8, 32, 256), precision=...]
    squeeze x6 -> x0, local copies, waits for them, and re-layouts: 26.6 us -> none  [the longest x2 13.4 us: shards(): piece[:, 1]]
    unnamed x2 -> x0, matrix products: 13.6 us -> none
    another operation x2, local copies, waits for them, and re-layouts: 14.9 us -> 5.09 us  [shards(): spectral = jnp.stack([low, spec.reshape(64, 32, 256)])]
    dot_general x0 -> x1, local copies, waits for them, and re-layouts: none -> 8.45 us  [shards(): jnp.einsum('dhkl,dky->hly', gather, y_inv.reshape(8, 32, 256), precision=...]
  transfers between devices with their start and end apart: 8 -> 4, of which waited for: 6 -> 0; matrix products, arithmetic and copies ran while one was open for 4% -> 19% of each run, Pallas kernels for 0% -> 58%
where the time goes in v1:
time: 214 us; the launch traced here: 210 us
  Pallas kernels  123 us (57%)
  local copies, waits for them, and re-layouts  40.5 us (19%)
  matrix products  34.9 us (16%)
  starting transfers between devices  10.5 us (5%)
    pallas_call x1, Pallas kernels, spectral_call(): pl.pallas_call(spectral_kernel, out_shape=(jax.ShapeDtypeStruct((8, 2, 32...  123 us
    dot_general x1, matrix products, shards(): jnp.einsum('dhkl,dky->hly', gather, y_inv.reshape(8, 32, 256), precision=...  20.2 us
    dot_general x1, matrix products, shards(): jnp.einsum('oi,bixy->boxy', local_weight, grid_field, precision=highest)  14.7 us
    unnamed x17, local copies, waits for them, and re-layouts  13 us
    dot_general x1, local copies, waits for them, and re-layouts, shards(): jnp.einsum('dhkl,dky->hly', gather, y_inv.reshape(8, 32, 256), precision=...  8.45 us
    ppermute x2, starting transfers between devices, padded_2(): lax.ppermute(lax.slice_in_dim(block, 0, width, axis=dim), axis, backward)  6.43 us
    slice x3, local copies, waits for them, and re-layouts, padded_2(): lax.slice_in_dim(block, 0, width, axis=dim)  5.79 us
    another operation x2, local copies, waits for them, and re-layouts, shards(): spectral = jnp.stack([low, spec.reshape(64, 32, 256)])  5.09 us
  transfers between devices with their start and end apart: 4, of which 0 were waited for; matrix products, arithmetic and copies ran while one was open for 19% of the time, Pallas kernels for 58%

profile of v1, /device:TPU:1, one launch (start us, length us, event | category | flops | bytes accessed | tf_op | source)
XLA Modules:
  0.0 210.2 jit_solution(1205430906485589177)
XLA Ops:
  0.0 0.0 copy-start
  0.0 0.0 copy-start.1
  0.0 4.7 %copy.38 = f32[2,64,32,256]{3,1,2,0:T(8,128)S(1)} copy(f32[2,64,32,256]{3,2,1,0:T(8,128)} %param.11) | data formatting | bytes 8388608 | tf_op args[0]
  4.7 0.0 copy-start.3
  4.7 2.0 copy-done.3
  6.7 0.7 fusion.21
  7.5 5.1 %collective-permute-start = (f32[2,64,1,256]{3,1,2,0:T(8,128)}, f32[2,64,1,256]{3,1,2,0:T(8,128)S(1)}, u32[]{:S(2)}, u32[]{:S(2)}) collective-permute-start(f32[2,64,1,256]{3,1,2,0:T(8,128)} %get-tuple-element.11), channel_id=1, source_target_pairs={{8,0},{16,8},{24,16},{32,24},{40,32},{48,40},{56,48},{64,56},{72,6... | collective-permute-start | bytes 393224 | tf_op jit(solution)/shard_map/ppermute | solution.py:728
  12.6 2.2 %collective-permute-start.1 = (f32[2,64,1,256]{3,1,2,0:T(8,128)}, f32[2,64,1,256]{3,1,2,0:T(8,128)S(1)}, u32[]{:S(2)}, u32[]{:S(2)}) collective-permute-start(f32[2,64,1,256]{3,1,2,0:T(8,128)} %get-tuple-element.12), channel_id=1, source_target_pairs={{0,8},{8,16},{16,24},{24,32},{32,40},{40,48},{48,56},{56,64},{64,7... | collective-permute-start | bytes 393224 | tf_op jit(solution)/shard_map/ppermute | solution.py:725
  14.8 0.0 copy-done.1
  14.9 0.0 copy-start.2
  14.9 1.2 copy-done.2
  16.1 122.8 %spectral.1 = (f32[8,2,32,1024]{3,2,1,0:T(8,128)S(1)}, f32[2,4,4,2,32,256]{5,4,3,2,1,0:T(8,128)}) custom-call(f32[2,2,4,4,2,32,256]{6,5,4,3,2,1,0:T(8,128)} %bitcast.28, f32[4,16,64,128]{3,2,1,0:T(8,128)} %weight.1, bf16[8,2,256,256]{3,2,1,0:T(8,128)(2,1)} %constant.32.clone.t_xf, bf16[8,2,512,128]{3,2,1,0:T(8,128)(2,1)} %constant.33.clone.t_xi, ...), custom_call_target="tpu_custom_call" | custom-call | tf_op jit(solution)/shard_map/spectral/pallas_call | solution.py:704
  138.9 8.4 %dot_general.11 = f32[2,8,2,2,32,8,32]{4,3,2,1,6,0,5:T(2,128)} reshape(f32[2,1024,8,32]{1,3,0,2:T(8,128)S(1)} %bitcast.27) | data formatting | bytes 4194304 | tf_op jit(solution)/shard_map/dhkl,dky->hly/dot_general | solution.py:739
  147.3 1.0 dynamic-slice_convert_fusion
  148.4 0.0 collective-permute-done.1
  148.4 4.9 %constant_dynamic-update-slice_fusion.1 = f32[2,64,34,256]{3,1,2,0:T(8,128)S(1)} fusion(f32[2,64,34,256]{3,1,2,0:T(8,128)S(1)} %constant_dynamic-update-slice_fusion.2, f32[2,64,32,256]{3,2,1,0:T(8,128)} %param.11), kind=kLoop, calls=%fused_computation.27 | loop fusion | bytes 8388608
  153.3 0.0 collective-permute-done
  153.3 0.0 copy-start.4
  153.3 2.7 %fusion.20 = (f32[2,64,34,1]{3,1,2,0:T(8,128)}, f32[2,64,34,1]{3,1,2,0:T(8,128)S(1)}) fusion(f32[2,64,34,256]{3,1,2,0:T(8,128)S(1)} %constant_dynamic-update-slice_fusion), kind=kLoop, calls=%fused_computation.29 | loop fusion | bytes 69632 | tf_op jit(solution)/shard_map/slice | solution.py:728
  156.0 0.1 copy-done.4
  156.1 2.4 %copy.44 = f32[2,64,34,1]{1,0,3,2:T(2,128)S(1)} copy(f32[2,64,34,1]{3,1,2,0:T(8,128)} %get-tuple-element.9) | data formatting | bytes 34816 | tf_op jit(solution)/shard_map/slice | solution.py:728
  158.5 0.7 copy.46
  159.2 1.9 collective-permute-start.3
  161.1 1.3 collective-permute-start.2
  162.4 0.0 copy-start.5
  162.4 20.2 %fusion.16 = f32[2,2,8,2,32,256]{5,4,0,3,2,1:T(8,128)S(1)} fusion(f32[8,32,256,1,1,1,1]{2,1,0,6,5,4,3:T(8,128)S(1)} %bitcast.31, f32[2,8,2,2,32,8,32]{4,3,2,1,6,0,5:T(2,128)} %dot_general.11), kind=kOutput, calls=%fused_computation.22 | convolution fusion | flops 1610612736 | bytes 4456448 | tf_op jit(solution)/shard_map/dhkl,dky->hly/dot_general | solution.py:739
  182.6 0.0 copy-done.5
  182.7 2.5 %copy.37 = f32[1,64,32,256]{3,1,2,0:T(8,128)} copy(f32[1,64,32,256]{3,2,1,0:T(8,128)S(1)} %bitcast.30) | data formatting | bytes 4194304 | tf_op jit(solution)/shard_map/stack;reshape | solution.py:742
  185.2 0.2 copy.35
  185.4 0.0 copy-start.6
  185.4 2.6 %copy.36 = f32[1,64,32,256]{3,1,2,0:T(8,128)} copy(f32[1,64,32,256]{3,2,1,0:T(8,128)S(1)} %bitcast.29) | data formatting | bytes 4194304 | tf_op jit(solution)/shard_map/stack;reshape | solution.py:742
  188.0 0.0 collective-permute-done.2
  188.0 0.7 copy.45
  188.7 0.0 collective-permute-done.3
  188.7 2.1 %copy.47 = f32[2,64,34,1]{3,1,2,0:T(8,128)} copy(f32[2,64,34,1]{1,0,3,2:T(2,128)S(1)} %collective-permute-done.3) | data formatting | bytes 34816 | tf_op jit(solution)/shard_map/ppermute | solution.py:725
  190.9 0.0 copy-done
  190.9 0.0 copy-done.6
  190.9 14.7 %fusion.8 = f32[2,64,32,256]{3,1,2,0:T(8,128)S(1)} fusion(f32[2,64,32,256]{3,1,2,0:T(8,128)} %copy-done.3, f32[2,64,34,256]{3,1,2,0:T(8,128)} %copy-done.4, f32[2,64,34,1]{3,1,2,0:T(8,128)} %copy.47, f32[2,64,34,1]{3,1,2,0:T(8,128)S(1)} %copy.45, f32[2,64,1,256]{3,1,2,0:T(8,128)S(1)} %collective-permute-done.1, ...), kind=kOutput, calls=%fused_computation.9 | convolution fusion | flops 827326464 | bytes 17385472 | tf_op jit(solution)/shard_map/oi,bixy->boxy/dot_general | solution.py:751
  205.6 4.4 %copy.49 = f32[2,64,32,256]{3,2,1,0:T(8,128)} copy(f32[2,64,32,256]{3,1,2,0:T(8,128)S(1)} %fusion.8) | data formatting | bytes 8388608 | tf_op jit(solution)/shard_map/mul | solution.py:752
  (3 shorter events, 0.1 us)
Async XLA Ops:
  0.0 190.9 %copy-start = (f32[64,64]{1,0:T(8,128)S(1)}, f32[64,64]{1,0:T(8,128)}, u32[]{:S(2)}) copy-start(f32[64,64]{1,0:T(8,128)} %param.14) | copy-start | bytes 49156
  0.0 14.8 %copy-start.1 = (bf16[2,128,2048]{2,1,0:T(8,128)(2,1)S(1)}, bf16[2,128,2048]{2,1,0:T(8,128)(2,1)}, u32[]{:S(2)}) copy-start(bf16[2,128,2048]{2,1,0:T(8,128)(2,1)} %constant.37.clone.t_xai) | copy-start | bytes 3145732
  4.7 2.0 copy-start.3
  7.5 145.8 %collective-permute-start = (f32[2,64,1,256]{3,1,2,0:T(8,128)}, f32[2,64,1,256]{3,1,2,0:T(8,128)S(1)}, u32[]{:S(2)}, u32[]{:S(2)}) collective-permute-start(f32[2,64,1,256]{3,1,2,0:T(8,128)} %get-tuple-element.11), channel_id=1, source_target_pairs={{8,0},{16,8},{24,16},{32,24},{40,32},{48,40},{56,48},{64,56},{72,6... | collective-permute-start | bytes 393224 | tf_op jit(solution)/shard_map/ppermute | solution.py:728
  12.6 135.7 %collective-permute-start.1 = (f32[2,64,1,256]{3,1,2,0:T(8,128)}, f32[2,64,1,256]{3,1,2,0:T(8,128)S(1)}, u32[]{:S(2)}, u32[]{:S(2)}) collective-permute-start(f32[2,64,1,256]{3,1,2,0:T(8,128)} %get-tuple-element.12), channel_id=1, source_target_pairs={{0,8},{8,16},{16,24},{24,32},{32,40},{40,48},{48,56},{56,64},{64,7... | collective-permute-start | bytes 393224 | tf_op jit(solution)/shard_map/ppermute | solution.py:725
  14.9 1.2 copy-start.2
  153.3 2.8 %copy-start.4 = (f32[2,64,34,256]{3,1,2,0:T(8,128)}, f32[2,64,34,256]{3,1,2,0:T(8,128)S(1)}, u32[]{:S(2)}) copy-start(f32[2,64,34,256]{3,1,2,0:T(8,128)S(1)} %constant_dynamic-update-slice_fusion) | copy-start | bytes 13369348
  159.2 29.5 %collective-permute-start.3 = (f32[2,64,34,1]{1,0,3,2:T(2,128)S(1)}, f32[2,64,34,1]{1,0,3,2:T(2,128)S(1)}, u32[]{:S(2)}, u32[]{:S(2)}) collective-permute-start(f32[2,64,34,1]{1,0,3,2:T(2,128)S(1)} %copy.46), channel_id=1, source_target_pairs={{0,1},{1,2},{2,3},{3,4},{4,5},{5,6},{6,7},{8,9},{9,10},{10,11},{11... | collective-permute-start | bytes 52232 | tf_op jit(solution)/shard_map/ppermute | solution.py:725
  161.1 26.9 %collective-permute-start.2 = (f32[2,64,34,1]{1,0,3,2:T(2,128)S(1)}, f32[2,64,34,1]{1,0,3,2:T(2,128)S(1)}, u32[]{:S(2)}, u32[]{:S(2)}) collective-permute-start(f32[2,64,34,1]{1,0,3,2:T(2,128)S(1)} %copy.44), channel_id=1, source_target_pairs={{1,0},{2,1},{3,2},{4,3},{5,4},{6,5},{7,6},{9,8},{10,9},{11,10},{12... | collective-permute-start | bytes 52232 | tf_op jit(solution)/shard_map/ppermute | solution.py:728
  162.4 20.2 %copy-start.5 = (f32[2,4,4,2,32,256]{5,4,3,2,1,0:T(8,128)S(1)}, f32[2,4,4,2,32,256]{5,4,3,2,1,0:T(8,128)}, u32[]{:S(2)}) copy-start(f32[2,4,4,2,32,256]{5,4,3,2,1,0:T(8,128)} %get-tuple-element.8) | copy-start | bytes 6291460
  185.4 5.4 %copy-start.6 = (f32[32,256]{1,0:T(8,128)S(1)}, f32[32,256]{1,0:T(8,128)}, u32[]{:S(2)}) copy-start(f32[32,256]{1,0:T(8,128)} %param.12) | copy-start | bytes 98308

commit v2 on v1

--- a/solution.py
+++ b/solution.py
@@ -15,7 +15,6 @@
 MY = 128
 NX = 1024
 NY = 2048
-highest = lax.Precision.HIGHEST
 f32 = jnp.float32
 bf16 = jnp.bfloat16
 
@@ -74,7 +73,7 @@
         halves(np.stack(y_inv_b)),
         halves(x_all_fwd),
         halves(x_all_inv),
-        halves(np.stack(y_inv_a)),
+        halves(np.stack(y_inv_a)).reshape(8, 2, 8, 32, 256),
     ]
 
 
@@ -154,23 +153,37 @@
 
 def spectral_kernel(
     grid,
+    flat,
     weight,
+    local_weight,
+    coefficient,
     t_xf,
     t_xi,
     t_yf,
     t_yi,
     t_xaf,
     t_xai,
-    gather,
-    spec,
+    t_yia,
+    result,
     xf,
     xi,
     yf,
     yi,
+    yia,
     xaf,
     xai,
     w,
-    g0,
+    w_high,
+    w_low,
+    wide,
+    lw,
+    coef,
+    g,
+    u,
+    row_send,
+    row_recv,
+    col_send,
+    col_recv,
     part,
     ring,
     first,
@@ -191,6 +204,8 @@
     h3r,
     h2r,
     out1,
+    gather,
+    spec,
     load,
     s_p1,
     r_p1,
@@ -216,7 +231,12 @@
     r_q2,
     s_q1,
     r_q1,
+    s_row,
+    r_row,
+    s_col,
+    r_col,
     own,
+    done,
 ):
     at = Place()
     j, d = at.j, at.d
@@ -227,7 +247,7 @@
         )
 
     loads = [
-        pltpu.make_async_copy(grid.at[0], g0, load.at[0]),
+        pltpu.make_async_copy(flat.at[pl.ds(0, 64)], g.at[pl.ds(0, 64)], load.at[0]),
         pltpu.make_async_copy(t_yf.at[d], yf, load.at[1]),
         pltpu.make_async_copy(t_xf.at[at.y], xf.at[0], load.at[2]),
         pltpu.make_async_copy(t_xf.at[4 + at.x], xf.at[1], load.at[3]),
@@ -237,9 +257,23 @@
         pltpu.make_async_copy(t_xi.at[at.y], xi.at[0], load.at[7]),
         pltpu.make_async_copy(t_xi.at[4 + at.x], xi.at[1], load.at[8]),
         pltpu.make_async_copy(t_yi.at[d], yi, load.at[9]),
+        pltpu.make_async_copy(local_weight, lw, load.at[10]),
+        pltpu.make_async_copy(flat.at[pl.ds(64, 64)], g.at[pl.ds(64, 64)], load.at[11]),
+        pltpu.make_async_copy(coefficient, coef, load.at[12]),
+        pltpu.make_async_copy(t_yia.at[d], yia, load.at[13]),
     ]
     for copy in loads:
         copy.start()
+
+    pending = []
+
+    def finish():
+        for wait in pending:
+            wait()
+
+    def send(copy):
+        copy.start()
+        pending.append(copy.wait_send)
 
     barrier = pltpu.get_barrier_semaphore()
 
@@ -280,7 +314,7 @@
     for chunk in range(2):
         for r in (2, 6, 3, 7, 4, 5, 1):
             for axis in range(2):
-                p1(axis, chunk, r).start()
+                send(p1(axis, chunk, r))
         for axis in range(2):
             p1_own(axis, chunk).start()
 
@@ -295,7 +329,7 @@
                 own_of = t + tile
                 for core in range(2):
                     for low in range(2):
-                        rows.append(g0[low, own_of // 4, own_of % 4, core])
+                        rows.append(g[2 * own_of + core + 32 * low])
             block = split(jnp.concatenate(rows, axis=0))
             result = dot3((yf[0], yf[1]), block, NT)
             for e in range(8):
@@ -322,14 +356,100 @@
                 to = at.gy(direction * (hops - 1 - s))
                 part[to, half] = part[to, half] + ring[chain, s]
                 if s + 1 < hops:
-                    hop(chain, s + 1).start()
+                    send(hop(chain, s + 1))
 
     columns(0, 0)
     for chain in (0, 2):
-        hop(chain, 0).start()
+        send(hop(chain, 0))
     columns(1, 0)
     for chain in (1, 3):
-        hop(chain, 0).start()
+        send(hop(chain, 0))
+
+    def halo_row(k):
+        to = (j + 31 + 2 * k) % 32
+        return remote(row_send.at[k], row_recv.at[k], s_row.at[k], r_row.at[k], to, d)
+
+    def halo_col(k):
+        return remote(
+            col_send.at[k], col_recv.at[k], s_col.at[k], r_col.at[k], j, at.gy(2 * k - 1)
+        )
+
+    loads[11].wait()
+    for k in range(2):
+        row_send[k] = g[:, 31 * k, :]
+        send(halo_row(k))
+    edge = lax.broadcasted_iota(jnp.int32, (16, 256), 0) * 255
+    pick = jnp.where(lax.broadcasted_iota(jnp.int32, (16, 256), 1) == edge, 1.0, 0.0).astype(bf16)
+
+    def edges(k, carry):
+        high, low = split(g[pl.ds(8 * k, 8)].reshape(256, 256))
+        found = dot(pick, high, NT) + dot(pick, low, NT)
+        col_send[0, k] = found[0:1]
+        col_send[1, k] = found[1:2]
+        return carry
+
+    lax.fori_loop(0, 16, edges, 0)
+    for k in range(2):
+        send(halo_col(k))
+
+    loads[10].wait()
+    spread_row = lax.broadcasted_iota(jnp.int32, (512, 64), 0) // 8
+    repeat = jnp.where(
+        spread_row == lax.broadcasted_iota(jnp.int32, (512, 64), 1), 1.0, 0.0
+    ).astype(bf16)
+    for part_of, piece in enumerate(split(lw[...])):
+        tall = dot(repeat, piece, NN).astype(bf16)
+        for k in range(4):
+            block = dot(tall[128 * k : 128 * k + 128], repeat, NT)
+            same = (lax.broadcasted_iota(jnp.int32, (128, 512), 0) % 8) == (
+                lax.broadcasted_iota(jnp.int32, (128, 512), 1) % 8
+            )
+            wide[part_of, 128 * k : 128 * k + 128, :] = jnp.where(same, block, 0.0).astype(bf16)
+
+    def pointwise(k, carry):
+        sample, rest = k // 4, k % 4
+        first_row = pl.multiple_of(8 * rest, 8)
+        block = split(g[pl.ds(64 * sample, 64), pl.ds(first_row, 8), :].reshape(512, 256))
+        for half in range(2):
+            mine = (
+                wide[0, 256 * half : 256 * half + 256],
+                wide[1, 256 * half : 256 * half + 256],
+            )
+            u[pl.ds(64 * sample + 32 * half, 32), pl.ds(first_row, 8), :] = dot3(
+                mine, block, NN
+            ).reshape(32, 8, 256)
+        return carry
+
+    row_of = lax.broadcasted_iota(jnp.int32, (8, 32, 256), 1)
+    lane_of = lax.broadcasted_iota(jnp.int32, (256, 256), 1)
+
+    def stencil(k, carry):
+        here = pl.ds(8 * k, 8)
+        block = g[here]
+        square = block.reshape(256, 256)
+        has_up = jnp.where(j > 0, 1.0, 0.0)
+        has_down = jnp.where(j < 31, 1.0, 0.0)
+        has_left = jnp.where(d > 0, 1.0, 0.0)
+        has_right = jnp.where(d < 7, 1.0, 0.0)
+        up = pltpu.roll(square, 1, 0).reshape(8, 32, 256)
+        down = pltpu.roll(square, 255, 0).reshape(8, 32, 256)
+        above = (row_recv[1, here] * has_up)[:, None, :]
+        below = (row_recv[0, here] * has_down)[:, None, :]
+        up = jnp.where(row_of == 0, jnp.broadcast_to(above, up.shape), up)
+        down = jnp.where(row_of == 31, jnp.broadcast_to(below, up.shape), down)
+        sides = jnp.concatenate(
+            [
+                col_recv[1, k] * has_left,
+                col_recv[0, k] * has_right,
+                jnp.zeros((6, 256), f32),
+            ],
+            axis=0,
+        ).T
+        left = jnp.where(lane_of == 0, sides[:, 0:1], pltpu.roll(square, 1, 1))
+        right = jnp.where(lane_of == 255, sides[:, 1:2], pltpu.roll(square, 255, 1))
+        beside = (up + down) + (left + right).reshape(8, 32, 256)
+        u[here] = u[here] + coef[...][None] * (block - 0.25 * beside)
+        return carry
 
     loads[2].wait()
     loads[3].wait()
@@ -361,14 +481,16 @@
 
         lax.fori_loop(0, 2, one, 0)
 
+    lax.fori_loop(0, 4, pointwise, 0)
     collect(0)
+    lax.fori_loop(4, 8, pointwise, 0)
     for axis in range(2):
         forward_chunk(axis, 0)
     collect(1)
     for axis in range(2):
         forward_chunk(axis, 1)
         for r in (1, 3, 2):
-            p2(axis, r).start()
+            send(p2(axis, r))
     collect(2)
 
     for axis in range(2):
@@ -383,7 +505,7 @@
         return remote(z3.at[to], z3r.at[r], s_p3.at[r], r_p3.at[r], j, to)
 
     for r in (4, 3, 5, 2, 6, 1, 7):
-        p3(r).start()
+        send(p3(r))
     collect(3)
 
     lane = lax.broadcasted_iota(jnp.int32, (16, 128), 1)
@@ -394,9 +516,9 @@
         a_send[2 * t] = jnp.where(lane < 64, real, pltpu.roll(imag, 64, 1))
         a_send[2 * t + 1] = jnp.where(lane < 64, pltpu.roll(real, 64, 1), imag)
 
-    def spread_copy(send, recv, s_sem, r_sem, r):
+    def spread_copy(out, into, s_sem, r_sem, r):
         gx = at.gx(r)
-        return remote(send.at[gx], recv.at[j], s_sem.at[r], r_sem.at[r], gx, d)
+        return remote(out.at[gx], into.at[j], s_sem.at[r], r_sem.at[r], gx, d)
 
     def spread_start(*refs):
         def start(r, carry):
@@ -404,8 +526,14 @@
             return carry
 
         lax.fori_loop(1, 32, start, 0)
-        send, recv = refs[:2]
-        recv[j] = send[j]
+        out, into = refs[:2]
+        into[j] = out[j]
+
+        def sent(r, carry):
+            spread_copy(*refs, r).wait_send()
+            return carry
+
+        pending.append(lambda: lax.fori_loop(1, 32, sent, 0))
 
     def spread_wait(*refs):
         def wait(r, carry):
@@ -416,6 +544,17 @@
 
     a_refs = (a_send, a_recv, s_a, r_a)
     spread_start(*a_refs)
+
+    loads[5].wait()
+
+    def split_weight(k, carry):
+        here = pl.ds(pl.multiple_of(k * 256, 256), 256)
+        high, low = split(w[here])
+        w_high[here] = high
+        w_low[here] = low
+        return carry
+
+    lax.fori_loop(0, 16, split_weight, 0)
 
     for r in range(1, 8):
         p3(r).wait_recv()
@@ -428,9 +567,9 @@
 
     loads[4].wait()
     spread_wait(*a_refs)
-    turned = [quarters([a_recv[4 * u + v] for v in range(4)]) for u in range(8)]
+    turned = [quarters([a_recv[4 * tile + v] for v in range(4)]) for tile in range(8)]
     rows = jnp.concatenate(
-        [jnp.concatenate([turned[u][k] for u in range(8)], axis=1) for k in range(4)], axis=0
+        [jnp.concatenate([turned[tile][k] for tile in range(8)], axis=1) for k in range(4)], axis=0
     )
     both = dot3(split(rows), (xaf[0], xaf[1]), NN)
     for half in range(2):
@@ -444,31 +583,49 @@
 
     m_refs = (m_send, m_recv, s_m, r_m)
     spread_start(*m_refs)
-    loads[5].wait()
     spread_wait(*m_refs)
 
-    sign = jnp.where(lax.broadcasted_iota(jnp.int32, (8, 128), 1) < 64, -1.0, 1.0)
-
-    def mix(kx, carry):
-        held = m_recv[:, kx, :]
+    held = jnp.concatenate([m_recv[:, kx, :] for kx in range(4)], axis=0).T
+    lane16 = lax.broadcasted_iota(jnp.int32, (16, 128), 1)
+    quarter = lane16 // 32
+    ky_of = lax.broadcasted_iota(jnp.int32, (64, 128), 0) % 16
+    ky_lane = lax.broadcasted_iota(jnp.int32, (64, 128), 1) // 64
+    sign = jnp.where(lane16 < 64, -1.0, 1.0)
+    for kx in range(4):
+        rows = []
         for sample in range(2):
-            rows = []
-            for ky in range(16):
-                from_real = jnp.zeros((32, 128), f32)
-                from_imag = jnp.zeros((32, 128), f32)
-                for half in range(2):
-                    first_lane = (64 if sample == 0 else 0) + 32 * half + ky
-                    block = w[kx, ky, 32 * half : 32 * half + 32, :]
-                    from_real += held[:, first_lane : first_lane + 1] * block
-                    from_imag += held[:, first_lane + 16 : first_lane + 17] * block
-                from_real = (from_real[0:8] + from_real[8:16]) + (from_real[16:24] + from_real[24:32])
-                from_imag = (from_imag[0:8] + from_imag[8:16]) + (from_imag[16:24] + from_imag[24:32])
-                both = from_real + sign * pltpu.roll(from_imag, 64, 1)
-                rows.append(jnp.sum(both, axis=0, keepdims=True))
-            mixed[pl.ds(64 * sample + 16 * kx, 16), :] = jnp.concatenate(rows, axis=0)
-        return carry
-
-    lax.fori_loop(0, 4, mix, 0)
+            for ri in range(2):
+                base = 64 * (1 - sample) + 16 * ri
+                low, high = held[base : base + 16], held[base + 32 : base + 48]
+                moved = []
+                for v in range(4):
+                    shift = (32 * (v - kx)) % 128
+                    source = low if v % 2 == 0 else high
+                    moved.append(source if shift == 0 else pltpu.roll(source, shift, 1))
+                rows.append(
+                    jnp.where(
+                        quarter < 2,
+                        jnp.where(quarter == 0, moved[0], moved[1]),
+                        jnp.where(quarter == 2, moved[2], moved[3]),
+                    )
+                )
+        stacked = jnp.concatenate(rows, axis=0)
+        top = stacked.astype(bf16).astype(f32)
+        rest = stacked - top
+        wide_top = jnp.concatenate(
+            [jnp.where(ky_of == 2 * t + ky_lane, top, 0.0).astype(bf16) for t in range(8)], axis=1
+        )
+        wide_rest = jnp.concatenate(
+            [jnp.where(ky_of == 2 * t + ky_lane, rest, 0.0).astype(bf16) for t in range(8)], axis=1
+        )
+        here = pl.ds(1024 * kx, 1024)
+        product = dot3((wide_top, wide_rest), (w_high[here], w_low[here]), NN)
+        for sample in range(2):
+            from_real = product[32 * sample : 32 * sample + 16]
+            from_imag = product[32 * sample + 16 : 32 * sample + 32]
+            mixed[64 * sample + 16 * kx : 64 * sample + 16 * kx + 16, :] = (
+                from_real + sign * pltpu.roll(from_imag, 64, 1)
+            )
     turned_modes = mixed[...].T
     for k in range(4):
         n_send[:, k, :] = turned_modes[32 * k : 32 * k + 32]
@@ -485,46 +642,30 @@
             quarters([back[64 * sample + 16 * v : 64 * sample + 16 * v + 16] for v in range(4)])
         )
 
-    for axis in range(2):
-        for k in range(2):
-            h3[axis, k] = by_sample[1][2 * k + axis]
-
-    def q3(r):
-        return remote(h3, h3r.at[d], s_q3.at[r], r_q3.at[r], j, at.gy(r))
-
-    for r in (4, 3, 5, 2, 6, 1, 7):
-        q3(r).start()
-    h3r[d] = h3[...]
-
     full = dot3(split(jnp.concatenate(by_sample[0], axis=0)), (xai[0], xai[1]), NN)
     real, imag = full[0:32], full[32:64]
     g_real = real[:, :1024] - imag[:, 1024:]
     g_imag = real[:, 1024:] + imag[:, :1024]
-    for u in range(8):
-        here = slice(128 * u, 128 * u + 128)
+    for tile in range(8):
+        here = slice(128 * tile, 128 * tile + 128)
         pieces = quarters(
             [g_real[0:16, here], g_real[16:32, here], g_imag[0:16, here], g_imag[16:32, here]]
         )
         for v in range(4):
-            b_send[4 * u + v] = pieces[v]
+            b_send[4 * tile + v] = pieces[v]
     b_refs = (b_send, b_recv, s_b, r_b)
     spread_start(*b_refs)
 
-    for r in range(1, 8):
-        q3(r).wait_recv()
-
-    def q2(axis, r):
-        place, gx = at.across(axis, r)
-        mine = at.y if axis == 0 else at.x
-        return remote(
-            h3r.at[:, axis], h2r.at[axis, mine], s_q2.at[axis, r], r_q2.at[axis, r], gx, d
-        )
-
-    for r in (1, 3, 2):
-        for axis in range(2):
-            q2(axis, r).start()
-    h2r[0, at.y] = h3r[:, 0]
-    h2r[1, at.x] = h3r[:, 1]
+    for axis in range(2):
+        for k in range(2):
+            h3[axis, k] = by_sample[1][2 * k + axis]
+
+    def q3(r):
+        return remote(h3, h3r.at[d], s_q3.at[r], r_q3.at[r], j, at.gy(r))
+
+    for r in (4, 3, 5, 2, 6, 1, 7):
+        send(q3(r))
+    h3r[d] = h3[...]
 
     spread_wait(*b_refs)
     for t in range(16):
@@ -552,12 +693,27 @@
             if s < hops:
                 lap(chain, s).wait_recv()
                 if s + 1 < hops:
-                    lap(chain, s + 1).start()
+                    send(lap(chain, s + 1))
 
     for chain in range(4):
-        lap(chain, 0).start()
-    keep = pltpu.make_async_copy(part.at[d], gather.at[d], own.at[0, 0])
-    keep.start()
+        send(lap(chain, 0))
+    gather[d] = part[d]
+
+    for r in range(1, 8):
+        q3(r).wait_recv()
+
+    def q2(axis, r):
+        place, gx = at.across(axis, r)
+        mine = at.y if axis == 0 else at.x
+        return remote(
+            h3r.at[:, axis], h2r.at[axis, mine], s_q2.at[axis, r], r_q2.at[axis, r], gx, d
+        )
+
+    for r in (1, 3, 2):
+        for axis in range(2):
+            send(q2(axis, r))
+    h2r[0, at.y] = h3r[:, 0]
+    h2r[1, at.x] = h3r[:, 1]
 
     for k in range(7, 10):
         loads[k].wait()
@@ -602,53 +758,74 @@
 
         lax.fori_loop(0, 2, one, 0)
         for r in (2, 6, 3, 7, 4, 5, 1):
-            q1(axis, chunk, r).start()
+            send(q1(axis, chunk, r))
         q1_own(axis, chunk).start()
 
+    for k in range(2):
+        halo_row(k).wait_recv()
+        halo_col(k).wait_recv()
+    loads[12].wait()
+    loads[13].wait()
+    lax.fori_loop(0, 6, stencil, 0)
+    pass_on(0)
     for axis in range(2):
         for r in range(1, 4):
             q2(axis, r).wait_recv()
     for axis in range(2):
         inverse_chunk(axis, 0)
-    pass_on(0)
     for axis in range(2):
         inverse_chunk(axis, 1)
     pass_on(1)
+    lax.fori_loop(6, 16, stencil, 0)
+
+    def inverse_columns(half, offsets):
+        blocks = [at.gy(offset) for offset in offsets]
+        table = tuple(jnp.concatenate([yia[k, e] for e in blocks], axis=0) for k in range(2))
+
+        def one(k, carry):
+            lanes = pl.ds(pl.multiple_of(128 * k, 128), 128)
+            modes = jnp.concatenate([gather[e, half, :, lanes] for e in blocks], axis=0)
+            both = dot3(split(modes), table, TN)
+            first_channel = 2 * (8 * half + k)
+            for n, channel in enumerate((0, 32, 1, 33)):
+                u[first_channel + channel] = u[first_channel + channel] + both[32 * n : 32 * n + 32]
+            return carry
+
+        lax.fori_loop(0, 8, one, 0)
+
+    for half in range(2):
+        inverse_columns(half, (0, -1, 1, -2, 2))
     pass_on(2)
-    pass_on(3)
-    for chunk in range(2):
-        for axis in range(2):
+
+    def put(first_channel, count, k):
+        copy = pltpu.make_async_copy(
+            u.at[pl.ds(first_channel, count)], result.at[pl.ds(first_channel, count)], done.at[k]
+        )
+        copy.start()
+        pending.append(copy.wait)
+
+    for axis in range(2):
+        for chunk in range(2):
             for r in range(1, 8):
                 q1(axis, chunk, r).wait_recv()
             q1_own(axis, chunk).wait()
-    keep.wait()
-
-    for chunk in range(2):
-        for axis in range(2):
-            for r in range(1, 8):
-                p1(axis, chunk, r).wait_send()
-                q1(axis, chunk, r).wait_send()
-    for axis in range(2):
-        for r in range(1, 4):
-            p2(axis, r).wait_send()
-            q2(axis, r).wait_send()
-    for r in range(1, 8):
-        p3(r).wait_send()
-        q3(r).wait_send()
-    for chain in range(4):
-        for s in range(CHAINS[chain][2]):
-            hop(chain, s).wait_send()
-            lap(chain, s).wait_send()
-
-    def sent(r, carry):
-        for refs in (a_refs, m_refs, n_refs, b_refs):
-            spread_copy(*refs, r).wait_send()
-        return carry
-
-    lax.fori_loop(1, 32, sent, 0)
-
-
-def spectral_call(grid_field, spectral_weight, consts):
+
+        def add(k, carry):
+            here = pl.ds(64 + 32 * axis + 8 * k, 8)
+            u[here] = u[here] + spec[axis, k].reshape(8, 32, 256)
+            return carry
+
+        lax.fori_loop(0, 4, add, 0)
+        put(64 + 32 * axis, 32, axis)
+    pass_on(3)
+    for half in range(2):
+        inverse_columns(half, (-3, 3, 4))
+        put(16 * half, 16, 2 + 2 * half)
+        put(32 + 16 * half, 16, 3 + 2 * half)
+    finish()
+
+
+def spectral_call(grid_field, coefficient, spectral_weight, local_weight, consts):
     dma = pltpu.SemaphoreType.DMA
     vmem = pltpu.VMEM
     scratch = [
@@ -656,10 +833,21 @@
         vmem((2, 2, 512, 128), bf16),
         vmem((2, 256, 256), bf16),
         vmem((2, 256, 256), bf16),
+        vmem((2, 8, 32, 256), bf16),
         vmem((2, 1024, 256), bf16),
         vmem((2, 128, 2048), bf16),
-        vmem((4, 16, 64, 128), f32),
-        vmem((2, 4, 4, 2, 32, 256), f32),
+        vmem((4096, 128), f32),
+        vmem((4096, 128), bf16),
+        vmem((4096, 128), bf16),
+        vmem((2, 512, 512), bf16),
+        vmem((64, 64), f32),
+        vmem((32, 256), f32),
+        vmem((128, 32, 256), f32),
+        vmem((128, 32, 256), f32),
+        vmem((2, 128, 256), f32),
+        vmem((2, 128, 256), f32),
+        vmem((2, 16, 1, 256), f32),
+        vmem((2, 16, 1, 256), f32),
         vmem((8, 2, 32, 1024), f32),
         vmem((4, 4, 32, 1024), f32),
         vmem((2, 4, 8, 32, 256), f32),
@@ -680,7 +868,9 @@
         vmem((8, 2, 2, 16, 128), f32),
         vmem((2, 4, 8, 2, 16, 128), f32),
         vmem((2, 4, 8, 32, 256), f32),
-        dma((10,)),
+        vmem((8, 2, 32, 1024), f32),
+        vmem((2, 4, 4, 2, 32, 256), f32),
+        dma((14,)),
         dma((2, 2, 8)),
         dma((2, 2, 8)),
         dma((2, 4)),
@@ -698,58 +888,38 @@
         dma((2, 4)),
         dma((2, 2, 8)),
         dma((2, 2, 8)),
+        *[dma((2,)) for _ in range(4)],
         dma((2, 4)),
+        dma((6,)),
     ]
     hbm = pl.BlockSpec(memory_space=pl.ANY)
     return pl.pallas_call(
         spectral_kernel,
-        out_shape=(
-            jax.ShapeDtypeStruct((8, 2, 32, 1024), f32),
-            jax.ShapeDtypeStruct((2, 4, 4, 2, 32, 256), f32),
-        ),
-        in_specs=[hbm] * 8,
-        out_specs=(hbm, hbm),
+        out_shape=jax.ShapeDtypeStruct((128, 32, 256), f32),
+        in_specs=[hbm] * 12,
+        out_specs=hbm,
         scratch_shapes=scratch,
         compiler_params=pltpu.CompilerParams(
-            collective_id=0, has_side_effects=True, vmem_limit_bytes=48 << 20
+            collective_id=0, has_side_effects=True, vmem_limit_bytes=56 << 20
         ),
         name="spectral",
-    )(grid_field, spectral_weight, *consts)
-
-
-def padded_2(block, sides, width):
-    for axis, dim in sides:
-        count = lax.axis_size(axis)
-        forward = [(i, i + 1) for i in range(count - 1)]
-        backward = [(target, source) for source, target in forward]
-        low = lax.ppermute(
-            lax.slice_in_dim(block, block.shape[dim] - width, None, axis=dim), axis, forward
-        )
-        high = lax.ppermute(lax.slice_in_dim(block, 0, width, axis=dim), axis, backward)
-        block = jnp.concatenate([low, block, high], axis=dim)
-    return block
-
-
-def shards(consts, grid_field, coefficient, spectral_weight, local_weight):
+    )(
+        grid_field.reshape(2, 2, 4, 4, 2, 32, 256),
+        grid_field.reshape(128, 32, 256),
+        spectral_weight.reshape(4096, 128),
+        local_weight,
+        coefficient,
+        *consts,
+    )
+
+
+def kernel_only(consts, grid_field, coefficient, spectral_weight, local_weight):
     consts = [jnp.asarray(c) for c in consts]
-    view = grid_field.reshape(2, 2, 4, 4, 2, 32, 256)
-    gather, spec = spectral_call(view, spectral_weight, consts[:6])
-    y_inv = consts[6][lax.axis_index("gy")].astype(f32)
-    y_inv = y_inv[0] + y_inv[1]
-    low = jnp.einsum("dhkl,dky->hly", gather, y_inv.reshape(8, 32, 256), precision=highest)
-    low = low.reshape(2, 8, 2, 2, 32, 256)
-    low = jnp.transpose(low, (3, 0, 1, 2, 4, 5)).reshape(64, 32, 256)
-    spectral = jnp.stack([low, spec.reshape(64, 32, 256)])
-    padded = padded_2(grid_field, (("gx", 2), ("gy", 3)), 1)
-    beside_all = (
-        padded[:, :, 2:, 1:-1]
-        + padded[:, :, :-2, 1:-1]
-        + padded[:, :, 1:-1, 2:]
-        + padded[:, :, 1:-1, :-2]
-    )
-    stencil = coefficient * (grid_field - 0.25 * beside_all)
-    pointwise = jnp.einsum("oi,bixy->boxy", local_weight, grid_field, precision=highest)
-    return jax.nn.gelu(spectral + pointwise + stencil)
+    return spectral_call(grid_field, coefficient, spectral_weight, local_weight, consts)
+
+
+def shards(consts, *arguments):
+    return jax.nn.gelu(kernel_only(consts, *arguments).reshape(2, 64, 32, 256))
 
 
 def solution(mesh):

time: 214 us -> 107 us (0.50); the launches traced: 210 us -> 107 us
  local copies, waits for them, and re-layouts: 40.5 us -> 0 us
  matrix products: 34.9 us -> 0 us
  Pallas kernels: 123 us -> 101 us
  starting transfers between devices: 10.5 us -> 0 us
  other arithmetic: 1.02 us -> 5.42 us
    dot_general x2 -> x0, matrix products: 34.9 us -> none  [the longest x1 20.2 us: shards(): jnp.einsum('dhkl,dky->hly', gather, y_inv.reshape(8, 32, 256), precision=...]
    pallas_call x1, Pallas kernels: 123 us -> 101 us  [spectral_call(): pl.pallas_call(spectral_kernel, out_shape=jax.ShapeDtypeStruct((128, 32,...]
    unnamed x17 -> x0, local copies, waits for them, and re-layouts: 13 us -> none
    ppermute x4 -> x0, starting transfers between devices: 10.5 us -> none  [the longest x2 6.43 us: padded_2(): lax.ppermute(lax.slice_in_dim(block, 0, width, axis=dim), axis, backward)]
    dot_general x1 -> x0, local copies, waits for them, and re-layouts: 8.45 us -> none  [shards(): jnp.einsum('dhkl,dky->hly', gather, y_inv.reshape(8, 32, 256), precision=...]
    slice x4 -> x0, local copies, waits for them, and re-layouts: 6.53 us -> none  [the longest x3 5.79 us: padded_2(): lax.slice_in_dim(block, 0, width, axis=dim)]
    mul x0 -> x1, other arithmetic: none -> 5.42 us  [shards(): return jax.nn.gelu(kernel_only(consts, *arguments).reshape(2, 64, 32, 256))]
    another operation x2 -> x0, local copies, waits for them, and re-layouts: 5.09 us -> none  [shards(): spectral = jnp.stack([low, spec.reshape(64, 32, 256)])]
  transfers between devices with their start and end apart: 4 -> 0, of which waited for: 0 -> 0; matrix products, arithmetic and copies ran while one was open for 19% -> 0% of each run, Pallas kernels for 58% -> 0%
where the time goes in v2:
time: 107 us
  Pallas kernels  101 us (94%)
  other arithmetic  5.42 us (5%)
    pallas_call x1, Pallas kernels, spectral_call(): pl.pallas_call(spectral_kernel, out_shape=jax.ShapeDtypeStruct((128, 32,...  101 us
    mul x1, other arithmetic, shards(): return jax.nn.gelu(kernel_only(consts, *arguments).reshape(2, 64, 32, 256))  5.42 us

profile of v2, /device:TPU:1, one launch (start us, length us, event | category | flops | bytes accessed | tf_op | source)
XLA Modules:
  0.0 106.7 jit_solution(2359402600274649490)
XLA Ops:
  0.0 101.2 %spectral.1 = f32[128,32,256]{2,1,0:T(8,128)} custom-call(f32[2,2,4,4,2,32,256]{6,5,4,3,2,1,0:T(8,128)} %bitcast.5, f32[128,32,256]{2,1,0:T(8,128)} %bitcast.6, f32[4096,128]{1,0:T(8,128)} %bitcast.7, f32[64,64]{1,0:T(8,128)} %local_weight.1, f32[32,256]{1,0:T(8,128)} %coefficient.1, bf16[8,2,256,256]{3,2,1,0:T(8,128)(2,1)} %constant.22.clone.t_xf, ...), custom_call_target="tpu_custom_call" | custom-call | tf_op jit(solution)/shard_map/spectral/pallas_call | solution.py:896
  101.3 5.4 %fusion.6 = f32[2,64,32,256]{3,2,1,0:T(8,128)} fusion(f32[2,64,32,256]{3,2,1,0:T(8,128)} %bitcast.4), kind=kLoop, calls=%fused_computation.7 | loop fusion | flops 8388608 | bytes 8388608 | tf_op jit(solution)/shard_map/mul | solution.py:922

commit v3 on v2

--- a/solution.py
+++ b/solution.py
@@ -92,7 +92,9 @@
 
 
 def dot3(a, b, dims):
-    return dot(a[0], b[0], dims) + (dot(a[0], b[1], dims) + dot(a[1], b[0], dims))
+    left = jnp.concatenate([a[0], a[1], a[0]], axis=dims[0][0])
+    right = jnp.concatenate([b[0], b[0], b[1]], axis=dims[1][0])
+    return dot(left, right, dims)
 
 
 def quarters(blocks):
@@ -116,36 +118,31 @@
         self.y = self.j // 8
         self.x = (self.j // 2) % 4
         self.c = self.j % 2
+        self.ys = [self.y] + [(self.y + k) % 4 for k in range(1, 4)]
+        self.xs = [self.x] + [(self.x + k) % 4 for k in range(1, 4)]
+        self.cs = [self.c, 1 - self.c]
+        self.ds = [self.d] + [(self.d + k) % 8 for k in range(1, 8)]
 
     def gx(self, r):
-        return (
-            ((self.y + r // 8) % 4) * 8 + ((self.x + (r // 2) % 4) % 4) * 2 + (self.c + r % 2) % 2
-        )
-
-    def gx_back(self, r):
-        return (
-            ((self.y + 4 - r // 8) % 4) * 8
-            + ((self.x + 4 - (r // 2) % 4) % 4) * 2
-            + (self.c + r % 2) % 2
-        )
+        return self.ys[r // 8] * 8 + self.xs[(r // 2) % 4] * 2 + self.cs[r % 2]
 
     def member(self, axis, r):
-        core = (self.c + r % 2) % 2
+        core = self.cs[r % 2]
         if axis == 0:
-            place = (self.x + r // 2) % 4
+            place = self.xs[r // 2]
             return place, core, self.y * 8 + place * 2 + core
-        place = (self.y + r // 2) % 4
+        place = self.ys[r // 2]
         return place, core, place * 8 + self.x * 2 + core
 
     def across(self, axis, r):
         if axis == 0:
-            place = (self.y + r) % 4
+            place = self.ys[r % 4]
             return place, place * 8 + self.x * 2 + self.c
-        place = (self.x + r) % 4
+        place = self.xs[r % 4]
         return place, self.y * 8 + place * 2 + self.c
 
     def gy(self, r):
-        return (self.d + r + 8) % 8
+        return self.ds[r % 8]
 
 
 CHAINS = ((1, 0, 4), (-1, 1, 4), (-1, 0, 3), (1, 1, 3))
@@ -197,7 +194,6 @@
     m_recv,
     n_send,
     n_recv,
-    mixed,
     b_send,
     b_recv,
     h3,
@@ -262,61 +258,67 @@
         pltpu.make_async_copy(coefficient, coef, load.at[12]),
         pltpu.make_async_copy(t_yia.at[d], yia, load.at[13]),
     ]
-    for copy in loads:
+    for k in (0, 1):
+        loads[k].start()
+
+    pending = []
+
+    def send(copy, alone=True):
         copy.start()
-
-    pending = []
-
-    def finish():
+        if alone:
+            pending.append(copy.wait_send)
+
+    def bytes_of(ref, sem):
+        return pltpu.make_async_copy(ref, ref, sem)
+
+    def drain():
         for wait in pending:
             wait()
-
-    def send(copy):
-        copy.start()
-        pending.append(copy.wait_send)
+        pending.clear()
 
     barrier = pltpu.get_barrier_semaphore()
 
-    def greet(r, carry):
+    for r in range(1, 32):
         pl.semaphore_signal(barrier, inc=1, device_id=(at.gx(r), d), device_id_type=MESH)
-        return carry
-
-    lax.fori_loop(1, 32, greet, 0)
     for r in range(1, 8):
         pl.semaphore_signal(barrier, inc=1, device_id=(j, at.gy(r)), device_id_type=MESH)
     pl.semaphore_wait(barrier, 31 + 7)
 
-    def grid_piece(axis, chunk, place, core):
+    FAR_FIRST = (2, 6, 3, 7, 4, 5, 1)
+
+    def grid_piece(axis, r, place, core):
         if axis == 0:
-            return grid.at[1, 0, pl.ds(2 * chunk, 2), place, core]
-        return grid.at[1, 1, place, pl.ds(2 * chunk, 2), core]
-
-    def p1(axis, chunk, r):
-        place, core, gx = at.member(axis, r)
+            return grid.at[1, 0, at.ys[r], place, core]
+        return grid.at[1, 1, place, at.xs[r], core]
+
+    def p1(axis, r, m):
+        place, core, gx = at.member(axis, m)
         mine = (at.x if axis == 0 else at.y) * 2 + at.c
         return remote(
-            grid_piece(axis, chunk, place, core),
-            first.at[axis, pl.ds(2 * chunk, 2), mine],
-            s_p1.at[axis, chunk, r],
-            r_p1.at[axis, chunk, r],
+            grid_piece(axis, r, place, core),
+            first.at[axis, at.across(axis, r)[0], mine],
+            s_p1.at[axis],
+            r_p1.at[axis, r],
             gx,
             d,
         )
 
-    def p1_own(axis, chunk):
+    def p1_own(axis, r):
         place = at.x if axis == 0 else at.y
         return pltpu.make_async_copy(
-            grid_piece(axis, chunk, place, at.c),
-            first.at[axis, pl.ds(2 * chunk, 2), place * 2 + at.c],
-            own.at[axis, chunk],
-        )
-
-    for chunk in range(2):
-        for r in (2, 6, 3, 7, 4, 5, 1):
+            grid_piece(axis, r, place, at.c),
+            first.at[axis, at.across(axis, r)[0], place * 2 + at.c],
+            own.at[axis, r],
+        )
+
+    def p1_start(r):
+        for m in FAR_FIRST:
             for axis in range(2):
-                send(p1(axis, chunk, r))
+                send(p1(axis, r, m), alone=False)
         for axis in range(2):
-            p1_own(axis, chunk).start()
+            p1_own(axis, r).start()
+
+    p1_start(2)
 
     loads[0].wait()
     loads[1].wait()
@@ -336,34 +338,43 @@
                 part[e, half, :, 256 * k : 256 * k + 256] = result[32 * e : 32 * e + 32]
         return carry
 
-    def hop(chain, s):
+    def hop(chain, s, piece):
         direction, half, hops = CHAINS[chain]
         to = at.gy(direction * (hops - s))
         return remote(
-            part.at[to, half],
-            ring.at[chain, s],
-            s_ring.at[chain, s],
-            r_ring.at[chain, s],
+            part.at[to, half, pl.ds(16 * piece, 16)],
+            ring.at[chain, s, pl.ds(16 * piece, 16)],
+            s_ring.at[0],
+            r_ring.at[chain, s, piece],
             j,
             at.gy(direction),
         )
 
     def collect(s):
-        for chain in range(4):
-            direction, half, hops = CHAINS[chain]
-            if s < hops:
-                hop(chain, s).wait_recv()
-                to = at.gy(direction * (hops - 1 - s))
-                part[to, half] = part[to, half] + ring[chain, s]
-                if s + 1 < hops:
-                    send(hop(chain, s + 1))
+        for piece in range(2):
+            for chain in range(4):
+                direction, half, hops = CHAINS[chain]
+                if s < hops:
+                    hop(chain, s, piece).wait_recv()
+                    to = at.gy(direction * (hops - 1 - s))
+                    rows = slice(16 * piece, 16 * piece + 16)
+                    part[to, half, rows] = part[to, half, rows] + ring[chain, s, rows]
+                    if s + 1 < hops:
+                        send(hop(chain, s + 1, piece), alone=False)
 
     columns(0, 0)
-    for chain in (0, 2):
-        send(hop(chain, 0))
+    for piece in range(2):
+        for chain in (0, 2):
+            send(hop(chain, 0, piece), alone=False)
     columns(1, 0)
-    for chain in (1, 3):
-        send(hop(chain, 0))
+    for piece in range(2):
+        for chain in (1, 3):
+            send(hop(chain, 0, piece), alone=False)
+
+    for r in (1, 3, 0):
+        p1_start(r)
+    for k in (2, 3, 4, 5, 10, 11, 12, 6, 13, 9, 7, 8):
+        loads[k].start()
 
     def halo_row(k):
         to = (j + 31 + 2 * k) % 32
@@ -374,37 +385,38 @@
             col_send.at[k], col_recv.at[k], s_col.at[k], r_col.at[k], j, at.gy(2 * k - 1)
         )
 
-    loads[11].wait()
-    for k in range(2):
-        row_send[k] = g[:, 31 * k, :]
-        send(halo_row(k))
-    edge = lax.broadcasted_iota(jnp.int32, (16, 256), 0) * 255
-    pick = jnp.where(lax.broadcasted_iota(jnp.int32, (16, 256), 1) == edge, 1.0, 0.0).astype(bf16)
-
-    def edges(k, carry):
-        high, low = split(g[pl.ds(8 * k, 8)].reshape(256, 256))
-        found = dot(pick, high, NT) + dot(pick, low, NT)
-        col_send[0, k] = found[0:1]
-        col_send[1, k] = found[1:2]
-        return carry
-
-    lax.fori_loop(0, 16, edges, 0)
-    for k in range(2):
-        send(halo_col(k))
-
-    loads[10].wait()
-    spread_row = lax.broadcasted_iota(jnp.int32, (512, 64), 0) // 8
-    repeat = jnp.where(
-        spread_row == lax.broadcasted_iota(jnp.int32, (512, 64), 1), 1.0, 0.0
-    ).astype(bf16)
-    for part_of, piece in enumerate(split(lw[...])):
-        tall = dot(repeat, piece, NN).astype(bf16)
-        for k in range(4):
-            block = dot(tall[128 * k : 128 * k + 128], repeat, NT)
-            same = (lax.broadcasted_iota(jnp.int32, (128, 512), 0) % 8) == (
-                lax.broadcasted_iota(jnp.int32, (128, 512), 1) % 8
-            )
-            wide[part_of, 128 * k : 128 * k + 128, :] = jnp.where(same, block, 0.0).astype(bf16)
+    def halos():
+        for k in range(2):
+            row_send[k] = g[:, 31 * k, :]
+            send(halo_row(k))
+        edge = lax.broadcasted_iota(jnp.int32, (16, 256), 0) * 255
+        pick = jnp.where(lax.broadcasted_iota(jnp.int32, (16, 256), 1) == edge, 1.0, 0.0).astype(bf16)
+
+        def edges(k, carry):
+            high, low = split(g[pl.ds(8 * k, 8)].reshape(256, 256))
+            found = dot(pick, high, NT) + dot(pick, low, NT)
+            col_send[0, k] = found[0:1]
+            col_send[1, k] = found[1:2]
+            return carry
+
+        lax.fori_loop(0, 16, edges, 0)
+        for k in range(2):
+            send(halo_col(k))
+
+    def widen():
+        loads[10].wait()
+        spread_row = lax.broadcasted_iota(jnp.int32, (512, 64), 0) // 8
+        repeat = jnp.where(
+            spread_row == lax.broadcasted_iota(jnp.int32, (512, 64), 1), 1.0, 0.0
+        ).astype(bf16)
+        for part_of, piece in enumerate(split(lw[...])):
+            tall = dot(repeat, piece, NN).astype(bf16)
+            for k in range(4):
+                block = dot(tall[128 * k : 128 * k + 128], repeat, NT)
+                same = (lax.broadcasted_iota(jnp.int32, (128, 512), 0) % 8) == (
+                    lax.broadcasted_iota(jnp.int32, (128, 512), 1) % 8
+                )
+                wide[part_of, 128 * k : 128 * k + 128, :] = jnp.where(same, block, 0.0).astype(bf16)
 
     def pointwise(k, carry):
         sample, rest = k // 4, k % 4
@@ -470,28 +482,26 @@
             z2.at[axis, place], z2r.at[axis, r], s_p2.at[axis, r], r_p2.at[axis, r], gx, d
         )
 
-    def forward_chunk(axis, chunk):
-        for r in range(1, 8):
-            p1(axis, chunk, r).wait_recv()
-        p1_own(axis, chunk).wait()
-
-        def one(k, carry):
-            modes_of(axis, 2 * chunk + k)
-            return carry
-
-        lax.fori_loop(0, 2, one, 0)
-
-    lax.fori_loop(0, 4, pointwise, 0)
+    def forward_channel(r):
+        for axis in range(2):
+            bytes_of(first.at[axis, at.across(axis, r)[0], pl.ds(0, 7)], r_p1.at[axis, r]).wait()
+            p1_own(axis, r).wait()
+            modes_of(axis, at.across(axis, r)[0])
+            if r:
+                send(p2(axis, r))
+
+    widen()
+    lax.fori_loop(0, 1, pointwise, 0)
+    forward_channel(2)
+    lax.fori_loop(1, 2, pointwise, 0)
+    forward_channel(1)
     collect(0)
-    lax.fori_loop(4, 8, pointwise, 0)
-    for axis in range(2):
-        forward_chunk(axis, 0)
+    forward_channel(3)
+    lax.fori_loop(2, 4, pointwise, 0)
+    loads[11].wait()
+    forward_channel(0)
+    lax.fori_loop(4, 6, pointwise, 0)
     collect(1)
-    for axis in range(2):
-        forward_chunk(axis, 1)
-        for r in (1, 3, 2):
-            send(p2(axis, r))
-    collect(2)
 
     for axis in range(2):
         for r in range(1, 4):
@@ -500,12 +510,37 @@
         for e in range(8):
             z3[e, axis] = (z2[axis, place, e] + z2r[axis, 1, e]) + (z2r[axis, 2, e] + z2r[axis, 3, e])
 
-    def p3(r):
-        to = at.gy(r)
-        return remote(z3.at[to], z3r.at[r], s_p3.at[r], r_p3.at[r], j, to)
-
-    for r in (4, 3, 5, 2, 6, 1, 7):
-        send(p3(r))
+    def p3(chain, s):
+        direction, axis, hops = CHAINS[chain]
+        to = at.gy(direction * (hops - s))
+        return remote(
+            z3.at[to, axis], z3r.at[chain, s], s_p3.at[chain, s], r_p3.at[chain, s], j, at.gy(direction)
+        )
+
+    def collect_modes(s):
+        for chain in range(4):
+            direction, axis, hops = CHAINS[chain]
+            if s < hops:
+                p3(chain, s).wait_recv()
+                to = at.gy(direction * (hops - 1 - s))
+                z3[to, axis] = z3[to, axis] + z3r[chain, s]
+                if s + 1 < hops:
+                    send(p3(chain, s + 1))
+
+    for chain in range(4):
+        send(p3(chain, 0))
+    halos()
+    collect_modes(0)
+    collect(2)
+    lax.fori_loop(6, 8, pointwise, 0)
+    collect_modes(1)
+    for k in range(2):
+        halo_row(k).wait_recv()
+        halo_col(k).wait_recv()
+    loads[12].wait()
+    lax.fori_loop(0, 4, stencil, 0)
+    collect_modes(2)
+    lax.fori_loop(4, 8, stencil, 0)
     collect(3)
 
     lane = lax.broadcasted_iota(jnp.int32, (16, 128), 1)
@@ -518,29 +553,19 @@
 
     def spread_copy(out, into, s_sem, r_sem, r):
         gx = at.gx(r)
-        return remote(out.at[gx], into.at[j], s_sem.at[r], r_sem.at[r], gx, d)
-
-    def spread_start(*refs):
-        def start(r, carry):
-            spread_copy(*refs, r).start()
-            return carry
-
-        lax.fori_loop(1, 32, start, 0)
-        out, into = refs[:2]
+        return remote(out.at[gx], into.at[j], s_sem.at[0], r_sem.at[0], gx, d)
+
+    def all_of(ref, sem):
+        return pltpu.make_async_copy(ref.at[pl.ds(0, 31)], ref.at[pl.ds(0, 31)], sem.at[0])
+
+    def spread_start(out, into, s_sem, r_sem):
+        for r in range(1, 32):
+            spread_copy(out, into, s_sem, r_sem, 32 - r).start()
         into[j] = out[j]
-
-        def sent(r, carry):
-            spread_copy(*refs, r).wait_send()
-            return carry
-
-        pending.append(lambda: lax.fori_loop(1, 32, sent, 0))
-
-    def spread_wait(*refs):
-        def wait(r, carry):
-            spread_copy(*refs, r).wait_recv()
-            return carry
-
-        lax.fori_loop(1, 32, wait, 0)
+        pending.append(all_of(out, s_sem).wait)
+
+    def spread_wait(out, into, s_sem, r_sem):
+        all_of(into, r_sem).wait()
 
     a_refs = (a_send, a_recv, s_a, r_a)
     spread_start(*a_refs)
@@ -556,14 +581,19 @@
 
     lax.fori_loop(0, 16, split_weight, 0)
 
-    for r in range(1, 8):
-        p3(r).wait_recv()
-    stack = []
-    for axis in range(2):
-        total = z3[d, axis]
-        for r in range(1, 8):
-            total = total + z3r[r, axis]
-        stack.append(total.reshape(32, 128))
+    def to_owners(sample, stack):
+        modes = jnp.concatenate(stack + [jnp.zeros((64, 128), f32)], axis=0).T
+        for owner in range(32):
+            m_send[sample, owner] = modes[4 * owner : 4 * owner + 4]
+        spread_start(*m_refs[sample])
+
+    m_refs, n_refs = (
+        [tuple(ref.at[sample] for ref in refs) for sample in range(2)]
+        for refs in ((m_send, m_recv, s_m, r_m), (n_send, n_recv, s_n, r_n))
+    )
+
+    collect_modes(3)
+    to_owners(1, [z3[d, axis].reshape(32, 128) for axis in range(2)])
 
     loads[4].wait()
     spread_wait(*a_refs)
@@ -572,31 +602,28 @@
         [jnp.concatenate([turned[tile][k] for tile in range(8)], axis=1) for k in range(4)], axis=0
     )
     both = dot3(split(rows), (xaf[0], xaf[1]), NN)
+    stack = []
     for half in range(2):
         real = both[16 * half : 16 * half + 16]
         imag = both[32 + 16 * half : 32 + 16 * half + 16]
         stack.append(real[:, :128] + imag[:, 128:])
         stack.append(imag[:, :128] - real[:, 128:])
-    modes = jnp.concatenate(stack, axis=0).T
-    for owner in range(32):
-        m_send[owner] = modes[4 * owner : 4 * owner + 4]
-
-    m_refs = (m_send, m_recv, s_m, r_m)
-    spread_start(*m_refs)
-    spread_wait(*m_refs)
-
-    held = jnp.concatenate([m_recv[:, kx, :] for kx in range(4)], axis=0).T
+    to_owners(0, stack)
+
     lane16 = lax.broadcasted_iota(jnp.int32, (16, 128), 1)
     quarter = lane16 // 32
-    ky_of = lax.broadcasted_iota(jnp.int32, (64, 128), 0) % 16
-    ky_lane = lax.broadcasted_iota(jnp.int32, (64, 128), 1) // 64
+    ky_of = lax.broadcasted_iota(jnp.int32, (32, 128), 0) % 16
+    ky_lane = lax.broadcasted_iota(jnp.int32, (32, 128), 1) // 64
     sign = jnp.where(lane16 < 64, -1.0, 1.0)
-    for kx in range(4):
-        rows = []
-        for sample in range(2):
+
+    def mix(sample):
+        spread_wait(*m_refs[sample])
+        held = jnp.concatenate([m_recv[sample, :, kx, :] for kx in range(4)], axis=0).T
+        mixed = []
+        for kx in range(4):
+            rows = []
             for ri in range(2):
-                base = 64 * (1 - sample) + 16 * ri
-                low, high = held[base : base + 16], held[base + 32 : base + 48]
+                low, high = held[16 * ri : 16 * ri + 16], held[32 + 16 * ri : 48 + 16 * ri]
                 moved = []
                 for v in range(4):
                     shift = (32 * (v - kx)) % 128
@@ -609,38 +636,53 @@
                         jnp.where(quarter == 2, moved[2], moved[3]),
                     )
                 )
-        stacked = jnp.concatenate(rows, axis=0)
-        top = stacked.astype(bf16).astype(f32)
-        rest = stacked - top
-        wide_top = jnp.concatenate(
-            [jnp.where(ky_of == 2 * t + ky_lane, top, 0.0).astype(bf16) for t in range(8)], axis=1
-        )
-        wide_rest = jnp.concatenate(
-            [jnp.where(ky_of == 2 * t + ky_lane, rest, 0.0).astype(bf16) for t in range(8)], axis=1
-        )
-        here = pl.ds(1024 * kx, 1024)
-        product = dot3((wide_top, wide_rest), (w_high[here], w_low[here]), NN)
-        for sample in range(2):
-            from_real = product[32 * sample : 32 * sample + 16]
-            from_imag = product[32 * sample + 16 : 32 * sample + 32]
-            mixed[64 * sample + 16 * kx : 64 * sample + 16 * kx + 16, :] = (
-                from_real + sign * pltpu.roll(from_imag, 64, 1)
+            stacked = jnp.concatenate(rows, axis=0)
+            top = stacked.astype(bf16).astype(f32)
+            rest = stacked - top
+            wide_top, wide_rest = (
+                jnp.concatenate(
+                    [jnp.where(ky_of == 2 * t + ky_lane, x, 0.0).astype(bf16) for t in range(8)], axis=1
+                )
+                for x in (top, rest)
             )
-    turned_modes = mixed[...].T
-    for k in range(4):
-        n_send[:, k, :] = turned_modes[32 * k : 32 * k + 32]
-
-    n_refs = (n_send, n_recv, s_n, r_n)
-    spread_start(*n_refs)
+            here = pl.ds(1024 * kx, 1024)
+            product = dot3((wide_top, wide_rest), (w_high[here], w_low[here]), NN)
+            mixed.append(product[0:16] + sign * pltpu.roll(product[16:32], 64, 1))
+        mixed.append(jnp.zeros((64, 128), f32))
+        turned_modes = jnp.concatenate(mixed, axis=0).T
+        for k in range(4):
+            n_send[sample, :, k, :] = turned_modes[32 * k : 32 * k + 32]
+        spread_start(*n_refs[sample])
+
+    def unmix(sample):
+        spread_wait(*n_refs[sample])
+        back = jnp.concatenate([n_recv[sample, :, k, :] for k in range(4)], axis=0).T
+        return quarters([back[16 * v : 16 * v + 16] for v in range(4)])
+
+    mix(1)
+    lax.fori_loop(8, 11, stencil, 0)
+    mix(0)
+    by_sample = [None, unmix(1)]
+
+    for axis in range(2):
+        for k in range(2):
+            h3[axis, k] = by_sample[1][2 * k + axis]
+
+    def q3(r):
+        return remote(h3, h3r.at[d], s_q3.at[r], r_q3.at[r], j, at.gy(r))
+
+    for r in (4, 3, 5, 2, 6, 1, 7):
+        send(q3(r))
+    h3r[d] = h3[...]
+
+    lax.fori_loop(11, 14, stencil, 0)
+    drain()
+    for axis in range(2):
+        bytes_of(first.at[axis, :, pl.ds(0, 7)], s_p1.at[axis]).wait()
+    bytes_of(ring.at[pl.ds(0, 3)], s_ring.at[0]).wait()
+    bytes_of(ring.at[3, pl.ds(0, 2)], s_ring.at[0]).wait()
     loads[6].wait()
-    spread_wait(*n_refs)
-
-    back = jnp.concatenate([n_recv[:, k, :] for k in range(4)], axis=0).T
-    by_sample = []
-    for sample in range(2):
-        by_sample.append(
-            quarters([back[64 * sample + 16 * v : 64 * sample + 16 * v + 16] for v in range(4)])
-        )
+    by_sample[0] = unmix(0)
 
     full = dot3(split(jnp.concatenate(by_sample[0], axis=0)), (xai[0], xai[1]), NN)
     real, imag = full[0:32], full[32:64]
@@ -655,17 +697,23 @@
             b_send[4 * tile + v] = pieces[v]
     b_refs = (b_send, b_recv, s_b, r_b)
     spread_start(*b_refs)
-
-    for axis in range(2):
-        for k in range(2):
-            h3[axis, k] = by_sample[1][2 * k + axis]
-
-    def q3(r):
-        return remote(h3, h3r.at[d], s_q3.at[r], r_q3.at[r], j, at.gy(r))
-
-    for r in (4, 3, 5, 2, 6, 1, 7):
-        send(q3(r))
-    h3r[d] = h3[...]
+    lax.fori_loop(14, 16, stencil, 0)
+
+    for r in range(1, 8):
+        q3(r).wait_recv()
+
+    def q2(axis, r):
+        place, gx = at.across(axis, r)
+        mine = at.y if axis == 0 else at.x
+        return remote(
+            h3r.at[:, axis], h2r.at[axis, mine], s_q2.at[axis, r], r_q2.at[axis, r], gx, d
+        )
+
+    for r in (1, 3, 2):
+        for axis in range(2):
+            send(q2(axis, r))
+    h2r[0, at.y] = h3r[:, 0]
+    h2r[1, at.x] = h3r[:, 1]
 
     spread_wait(*b_refs)
     for t in range(16):
@@ -674,46 +722,32 @@
         part[d, t // 8, 0:16, here] = jnp.where(lane < 64, even, pltpu.roll(odd, 64, 1))
         part[d, t // 8, 16:32, here] = jnp.where(lane < 64, pltpu.roll(even, 64, 1), odd)
 
-    def lap(chain, s):
+    def lap(chain, s, piece):
         direction, half, hops = CHAINS[chain]
         block = at.gy(-direction * s)
-        src = part.at[block, half] if s == 0 else gather.at[block, half]
+        rows = pl.ds(16 * piece, 16)
         return remote(
-            src,
-            gather.at[block, half],
-            s_g.at[chain, s],
-            r_g.at[chain, s],
+            (part if s == 0 else gather).at[block, half, rows],
+            gather.at[block, half, rows],
+            s_g.at[0],
+            r_g.at[chain, s, piece],
             j,
             at.gy(direction),
         )
 
     def pass_on(s):
+        for piece in range(2):
+            for chain in range(4):
+                hops = CHAINS[chain][2]
+                if s < hops:
+                    lap(chain, s, piece).wait_recv()
+                    if s + 1 < hops:
+                        send(lap(chain, s + 1, piece), alone=False)
+
+    for piece in range(2):
         for chain in range(4):
-            hops = CHAINS[chain][2]
-            if s < hops:
-                lap(chain, s).wait_recv()
-                if s + 1 < hops:
-                    send(lap(chain, s + 1))
-
-    for chain in range(4):
-        send(lap(chain, 0))
+            send(lap(chain, 0, piece), alone=False)
     gather[d] = part[d]
-
-    for r in range(1, 8):
-        q3(r).wait_recv()
-
-    def q2(axis, r):
-        place, gx = at.across(axis, r)
-        mine = at.y if axis == 0 else at.x
-        return remote(
-            h3r.at[:, axis], h2r.at[axis, mine], s_q2.at[axis, r], r_q2.at[axis, r], gx, d
-        )
-
-    for r in (1, 3, 2):
-        for axis in range(2):
-            send(q2(axis, r))
-    h2r[0, at.y] = h3r[:, 0]
-    h2r[1, at.x] = h3r[:, 1]
 
     for k in range(7, 10):
         loads[k].wait()
@@ -727,102 +761,104 @@
         wide = split(jnp.concatenate([g_real, g_imag], axis=1))
         out1[axis, channel] = dot3(wide, (yi[0], yi[1]), NN).reshape(8, 32, 256)
 
-    def spec_piece(axis, chunk):
-        if axis == 0:
-            return spec.at[0, pl.ds(2 * chunk, 2), at.x, at.c]
-        return spec.at[1, at.y, pl.ds(2 * chunk, 2), at.c]
-
-    def q1(axis, chunk, r):
-        place, core, gx = at.member(axis, r)
+    def spec_piece(axis, r):
+        channel = at.across(axis, 4 - r)[0]
+        return spec.at[axis, channel, (at.x if axis == 0 else at.y) * 2 + at.c]
+
+    def q1(axis, r, m):
+        place, core, gx = at.member(axis, m)
         return remote(
-            out1.at[axis, pl.ds(2 * chunk, 2), place * 2 + core],
-            spec_piece(axis, chunk),
-            s_q1.at[axis, chunk, r],
-            r_q1.at[axis, chunk, r],
+            out1.at[axis, at.across(axis, 4 - r)[0], place * 2 + core],
+            spec_piece(axis, r),
+            s_q1.at[axis],
+            r_q1.at[axis],
             gx,
             d,
         )
 
-    def q1_own(axis, chunk):
+    def q1_own(axis, r):
         place = at.x if axis == 0 else at.y
         return pltpu.make_async_copy(
-            out1.at[axis, pl.ds(2 * chunk, 2), place * 2 + at.c],
-            spec_piece(axis, chunk),
-            own.at[axis, 2 + chunk],
-        )
-
-    def inverse_chunk(axis, chunk):
-        def one(k, carry):
-            rows_of(axis, 2 * chunk + k)
-            return carry
-
-        lax.fori_loop(0, 2, one, 0)
-        for r in (2, 6, 3, 7, 4, 5, 1):
-            send(q1(axis, chunk, r))
-        q1_own(axis, chunk).start()
-
-    for k in range(2):
-        halo_row(k).wait_recv()
-        halo_col(k).wait_recv()
-    loads[12].wait()
+            out1.at[axis, at.across(axis, 4 - r)[0], place * 2 + at.c],
+            spec_piece(axis, r),
+            own.at[axis, r],
+        )
+
+    def inverse_channel(r):
+        for axis in range(2):
+            if r:
+                q2(axis, r).wait_recv()
+            rows_of(axis, at.across(axis, 4 - r)[0])
+            for m in FAR_FIRST:
+                send(q1(axis, r, m), alone=False)
+            q1_own(axis, r).start()
+
+    inverse_channel(0)
+    inverse_channel(1)
+    inverse_channel(3)
+    pass_on(0)
+    inverse_channel(2)
     loads[13].wait()
-    lax.fori_loop(0, 6, stencil, 0)
-    pass_on(0)
-    for axis in range(2):
-        for r in range(1, 4):
-            q2(axis, r).wait_recv()
-    for axis in range(2):
-        inverse_chunk(axis, 0)
-    for axis in range(2):
-        inverse_chunk(axis, 1)
     pass_on(1)
-    lax.fori_loop(6, 16, stencil, 0)
-
-    def inverse_columns(half, offsets):
+
+    def inverse_columns(half, offsets, last=False):
         blocks = [at.gy(offset) for offset in offsets]
         table = tuple(jnp.concatenate([yia[k, e] for e in blocks], axis=0) for k in range(2))
 
         def one(k, carry):
-            lanes = pl.ds(pl.multiple_of(128 * k, 128), 128)
+            lanes = pl.ds(256 * k if last else pl.multiple_of(256 * k, 256), 256)
             modes = jnp.concatenate([gather[e, half, :, lanes] for e in blocks], axis=0)
             both = dot3(split(modes), table, TN)
-            first_channel = 2 * (8 * half + k)
-            for n, channel in enumerate((0, 32, 1, 33)):
+            first_channel = 2 * (8 * half + 2 * k)
+            for n, channel in enumerate((0, 32, 1, 33, 2, 34, 3, 35)):
                 u[first_channel + channel] = u[first_channel + channel] + both[32 * n : 32 * n + 32]
             return carry
 
-        lax.fori_loop(0, 8, one, 0)
+        if not last:
+            lax.fori_loop(0, 4, one, 0)
+            return
+        for k in range(4):
+            one(k, 0)
+            for low in range(2):
+                put(16 * half + 4 * k + 32 * low, 4, 2 + 8 * half + 2 * k + low)
+
+    def put(first_channel, count, k):
+        copy = pltpu.make_async_copy(
+            u.at[pl.ds(first_channel, count)], result.at[pl.ds(first_channel, count)], done.at[k]
+        )
+        copy.start()
+        pending.append(copy.wait)
 
     for half in range(2):
         inverse_columns(half, (0, -1, 1, -2, 2))
     pass_on(2)
-
-    def put(first_channel, count, k):
-        copy = pltpu.make_async_copy(
-            u.at[pl.ds(first_channel, count)], result.at[pl.ds(first_channel, count)], done.at[k]
-        )
-        copy.start()
-        pending.append(copy.wait)
-
+    for half in range(2):
+        inverse_columns(half, (-3, 3))
     for axis in range(2):
-        for chunk in range(2):
-            for r in range(1, 8):
-                q1(axis, chunk, r).wait_recv()
-            q1_own(axis, chunk).wait()
+        bytes_of(spec.at[axis, :, pl.ds(0, 7)], r_q1.at[axis]).wait()
+        for r in range(4):
+            q1_own(axis, r).wait()
 
         def add(k, carry):
-            here = pl.ds(64 + 32 * axis + 8 * k, 8)
-            u[here] = u[here] + spec[axis, k].reshape(8, 32, 256)
+            if axis == 0:
+                here = pl.ds(64 + 8 * k, 8)
+                u[here] = u[here] + spec[0, k]
+            else:
+                for place in range(4):
+                    here = pl.ds(96 + 8 * k + 2 * place, 2)
+                    u[here] = u[here] + spec[1, place, pl.ds(2 * k, 2)]
             return carry
 
         lax.fori_loop(0, 4, add, 0)
         put(64 + 32 * axis, 32, axis)
     pass_on(3)
     for half in range(2):
-        inverse_columns(half, (-3, 3, 4))
-        put(16 * half, 16, 2 + 2 * half)
-        put(32 + 16 * half, 16, 3 + 2 * half)
-    finish()
+        inverse_columns(half, (4,), last=True)
+    drain()
+    for axis in range(2):
+        bytes_of(out1.at[axis, :, pl.ds(0, 7)], s_q1.at[axis]).wait()
+    bytes_of(ring.at[pl.ds(0, 3)], s_g.at[0]).wait()
+    bytes_of(ring.at[3, pl.ds(0, 2)], s_g.at[0]).wait()
 
 
 def spectral_call(grid_field, coefficient, spectral_weight, local_weight, consts):
@@ -854,14 +890,13 @@
         vmem((2, 4, 8, 2, 16, 128), f32),
         vmem((2, 4, 8, 2, 16, 128), f32),
         vmem((8, 2, 2, 16, 128), f32),
-        vmem((8, 2, 2, 16, 128), f32),
+        vmem((4, 4, 2, 16, 128), f32),
         vmem((32, 16, 128), f32),
         vmem((32, 16, 128), f32),
-        vmem((32, 4, 128), f32),
-        vmem((32, 4, 128), f32),
-        vmem((32, 4, 128), f32),
-        vmem((32, 4, 128), f32),
-        vmem((128, 128), f32),
+        vmem((2, 32, 4, 128), f32),
+        vmem((2, 32, 4, 128), f32),
+        vmem((2, 32, 4, 128), f32),
+        vmem((2, 32, 4, 128), f32),
         vmem((32, 16, 128), f32),
         vmem((32, 16, 128), f32),
         vmem((2, 2, 16, 128), f32),
@@ -869,28 +904,30 @@
         vmem((2, 4, 8, 2, 16, 128), f32),
         vmem((2, 4, 8, 32, 256), f32),
         vmem((8, 2, 32, 1024), f32),
-        vmem((2, 4, 4, 2, 32, 256), f32),
+        vmem((2, 4, 8, 32, 256), f32),
         dma((14,)),
-        dma((2, 2, 8)),
-        dma((2, 2, 8)),
+        dma((2,)),
         dma((2, 4)),
         dma((2, 4)),
-        dma((8,)),
-        dma((8,)),
+        dma((2, 4)),
         dma((4, 4)),
         dma((4, 4)),
-        *[dma((32,)) for _ in range(8)],
-        dma((4, 4)),
-        dma((4, 4)),
+        dma((1,)),
+        dma((4, 4, 2)),
+        *[dma((1,)) for _ in range(2)],
+        *[dma((2, 1)) for _ in range(4)],
+        *[dma((1,)) for _ in range(2)],
+        dma((1,)),
+        dma((4, 4, 2)),
         dma((8,)),
         dma((8,)),
         dma((2, 4)),
         dma((2, 4)),
-        dma((2, 2, 8)),
-        dma((2, 2, 8)),
+        dma((2,)),
+        dma((2,)),
         *[dma((2,)) for _ in range(4)],
         dma((2, 4)),
-        dma((6,)),
+        dma((18,)),
     ]
     hbm = pl.BlockSpec(memory_space=pl.ANY)
     return pl.pallas_call(

time: 107 us -> 101 us (0.944)
  Pallas kernels: 101 us -> 95.3 us
    pallas_call x1, Pallas kernels: 101 us -> 95.3 us  [spectral_call(): pl.pallas_call(spectral_kernel, out_shape=jax.ShapeDtypeStruct((128, 32,...]
where the time goes in v3:
time: 101 us
  Pallas kernels  95.3 us (94%)
  other arithmetic  5.42 us (5%)
    pallas_call x1, Pallas kernels, spectral_call(): pl.pallas_call(spectral_kernel, out_shape=jax.ShapeDtypeStruct((128, 32,...  95.3 us
    mul x1, other arithmetic, shards(): return jax.nn.gelu(kernel_only(consts, *arguments).reshape(2, 64, 32, 256))  5.42 us

profile of v3, /device:TPU:1, one launch (start us, length us, event | category | flops | bytes accessed | tf_op | source)
XLA Modules:
  0.0 100.7 jit_solution(16376259491757044400)
XLA Ops:
  0.0 95.3 %spectral.1 = f32[128,32,256]{2,1,0:T(8,128)} custom-call(f32[2,2,4,4,2,32,256]{6,5,4,3,2,1,0:T(8,128)} %bitcast.5, f32[128,32,256]{2,1,0:T(8,128)} %bitcast.6, f32[4096,128]{1,0:T(8,128)} %bitcast.7, f32[64,64]{1,0:T(8,128)} %local_weight.1, f32[32,256]{1,0:T(8,128)} %coefficient.1, bf16[8,2,256,256]{3,2,1,0:T(8,128)(2,1)} %constant.22.clone.t_xf, ...), custom_call_target="tpu_custom_call" | custom-call | tf_op jit(solution)/shard_map/spectral/pallas_call | solution.py:933
  95.3 5.4 %fusion.6 = f32[2,64,32,256]{3,2,1,0:T(8,128)} fusion(f32[2,64,32,256]{3,2,1,0:T(8,128)} %bitcast.4), kind=kLoop, calls=%fused_computation.7 | loop fusion | flops 8388608 | bytes 8388608 | tf_op jit(solution)/shard_map/mul | solution.py:959

commit v4 on v3

--- a/solution.py
+++ b/solution.py
@@ -342,8 +342,8 @@
         direction, half, hops = CHAINS[chain]
         to = at.gy(direction * (hops - s))
         return remote(
-            part.at[to, half, pl.ds(16 * piece, 16)],
-            ring.at[chain, s, pl.ds(16 * piece, 16)],
+            part.at[to, half, pl.ds(0, 32)],
+            ring.at[chain, s, pl.ds(0, 32)],
             s_ring.at[0],
             r_ring.at[chain, s, piece],
             j,
@@ -351,23 +351,23 @@
         )
 
     def collect(s):
-        for piece in range(2):
+        for piece in range(1):
             for chain in range(4):
                 direction, half, hops = CHAINS[chain]
                 if s < hops:
                     hop(chain, s, piece).wait_recv()
                     to = at.gy(direction * (hops - 1 - s))
-                    rows = slice(16 * piece, 16 * piece + 16)
+                    rows = slice(0, 32)
                     part[to, half, rows] = part[to, half, rows] + ring[chain, s, rows]
                     if s + 1 < hops:
                         send(hop(chain, s + 1, piece), alone=False)
 
     columns(0, 0)
-    for piece in range(2):
+    for piece in range(1):
         for chain in (0, 2):
             send(hop(chain, 0, piece), alone=False)
     columns(1, 0)
-    for piece in range(2):
+    for piece in range(1):
         for chain in (1, 3):
             send(hop(chain, 0, piece), alone=False)
 
@@ -699,22 +699,6 @@
     spread_start(*b_refs)
     lax.fori_loop(14, 16, stencil, 0)
 
-    for r in range(1, 8):
-        q3(r).wait_recv()
-
-    def q2(axis, r):
-        place, gx = at.across(axis, r)
-        mine = at.y if axis == 0 else at.x
-        return remote(
-            h3r.at[:, axis], h2r.at[axis, mine], s_q2.at[axis, r], r_q2.at[axis, r], gx, d
-        )
-
-    for r in (1, 3, 2):
-        for axis in range(2):
-            send(q2(axis, r))
-    h2r[0, at.y] = h3r[:, 0]
-    h2r[1, at.x] = h3r[:, 1]
-
     spread_wait(*b_refs)
     for t in range(16):
         even, odd = b_recv[2 * t], b_recv[2 * t + 1]
@@ -725,7 +709,7 @@
     def lap(chain, s, piece):
         direction, half, hops = CHAINS[chain]
         block = at.gy(-direction * s)
-        rows = pl.ds(16 * piece, 16)
+        rows = pl.ds(0, 32)
         return remote(
             (part if s == 0 else gather).at[block, half, rows],
             gather.at[block, half, rows],
@@ -736,7 +720,7 @@
         )
 
     def pass_on(s):
-        for piece in range(2):
+        for piece in range(1):
             for chain in range(4):
                 hops = CHAINS[chain][2]
                 if s < hops:
@@ -744,10 +728,26 @@
                     if s + 1 < hops:
                         send(lap(chain, s + 1, piece), alone=False)
 
-    for piece in range(2):
+    for piece in range(1):
         for chain in range(4):
             send(lap(chain, 0, piece), alone=False)
     gather[d] = part[d]
+
+    for r in range(1, 8):
+        q3(r).wait_recv()
+
+    def q2(axis, r):
+        place, gx = at.across(axis, r)
+        mine = at.y if axis == 0 else at.x
+        return remote(
+            h3r.at[:, axis], h2r.at[axis, mine], s_q2.at[axis, r], r_q2.at[axis, r], gx, d
+        )
+
+    for r in (1, 3, 2):
+        for axis in range(2):
+            send(q2(axis, r))
+    h2r[0, at.y] = h3r[:, 0]
+    h2r[1, at.x] = h3r[:, 1]
 
     for k in range(7, 10):
         loads[k].wait()
@@ -955,8 +955,22 @@
     return spectral_call(grid_field, coefficient, spectral_weight, local_weight, consts)
 
 
+def gelu_kernel(sums, result):
+    result[...] = jax.nn.gelu(sums[...])
+
+
 def shards(consts, *arguments):
-    return jax.nn.gelu(kernel_only(consts, *arguments).reshape(2, 64, 32, 256))
+    block = pl.BlockSpec((32, 32, 256), lambda k: (k, 0, 0))
+    result = pl.pallas_call(
+        gelu_kernel,
+        grid=(4,),
+        in_specs=[block],
+        out_specs=block,
+        out_shape=jax.ShapeDtypeStruct((128, 32, 256), f32),
+        compiler_params=pltpu.CompilerParams(vmem_limit_bytes=56 << 20),
+        name="gelu",
+    )(kernel_only(consts, *arguments))
+    return result.reshape(2, 64, 32, 256)
 
 
 def solution(mesh):

time: 101 us -> 105 us (1.040)
  the two profiles are of different devices: /device:TPU:1 before, /device:TPU:2 now
where the time goes in v4:
time: 105 us
  Pallas kernels  105 us (100%)
    pallas_call x1, Pallas kernels, spectral_call(): pl.pallas_call(spectral_kernel, out_shape=jax.ShapeDtypeStruct((128, 32,...  99.6 us
    pallas_call x1, Pallas kernels, shards(): pl.pallas_call(gelu_kernel, grid=(4,), in_specs=[block], out_specs=block,...  5.18 us

profile of v4, /device:TPU:2, one launch (start us, length us, event | category | flops | bytes accessed | tf_op | source)
XLA Modules:
  0.0 104.8 jit_solution(1276615302272857337)
XLA Ops:
  0.0 99.6 %spectral.1.sums = f32[128,32,256]{2,1,0:T(8,128)} custom-call(f32[2,2,4,4,2,32,256]{6,5,4,3,2,1,0:T(8,128)} %bitcast.4, f32[128,32,256]{2,1,0:T(8,128)} %bitcast.5, f32[4096,128]{1,0:T(8,128)} %bitcast.6, f32[64,64]{1,0:T(8,128)} %local_weight.1, f32[32,256]{1,0:T(8,128)} %coefficient.1, bf16[8,2,256,256]{3,2,1,0:T(8,128)(2,1)} %constant.14.clone.t_xf, ...), custom_call_target="tpu_custom_call" | custom-call | tf_op jit(solution)/shard_map/spectral/pallas_call | solution.py:933
  99.6 5.2 %gelu.1 = f32[128,32,256]{2,1,0:T(8,128)} custom-call(f32[128,32,256]{2,1,0:T(8,128)} %spectral.1.sums), custom_call_target="tpu_custom_call" | custom-call | tf_op jit(solution)/shard_map/gelu/pallas_call | solution.py:964
